TPU v7x, 32 devices: a whole 2x2x4 slice. The times are simulated.
32 devices in a mesh: groups: 2 (over x), row: 16 (over z, y, core).
Axes of the slice: x: 2, y: 2, z: 4, core: 2. Of those that a mesh axis runs over, the one named last changes fastest.
Arguments:
- density_guess: bfloat16 [512, 128, 128], P(('groups', 'row')), parts along dimension 0, may hold values from -5 to 5
- cotangent: bfloat16 [512, 128, 128], P(('groups', 'row')), parts along dimension 0, may hold values from -6 to 6
- term_left: int32 [512, 4], P(('groups', 'row')), parts along dimension 0, may hold values from 0 to 15
- term_fetch: int32 [512, 4], P(('groups', 'row')), parts along dimension 0, may hold values from 0 to 31
- req_owner: int32 [1024, 1], P('groups'), parts along dimension 0, may hold values from 0 to 15; in each aligned block of 32 rows (0 to 31, 32 to 63, ...) at most 4 rows name the same one
- req_slot: int32 [1024], P('groups'), parts along dimension 0, may hold values from 0 to 15
Outputs:
- purified: bfloat16 [512, 128, 128], P(('groups', 'row')), parts along dimension 0
- guess_grad: float32 [512, 128, 128], P(('groups', 'row')), parts along dimension 0
There are 2 independent parts, one for each index of `groups`. A program takes and returns all parts, laid end to end along the dimension named above; each array names one. Nothing has to cross between parts.
Inputs may be any that keep to these rules, and one draw needn't show every extreme that they name: `req_owner`: among the 32 requests of one group, at most 4 name the same owner; in every draw some group names some owner exactly 4 times.
All inputs are finite; a program needn't handle non-finite values.
Results may differ from a plain program's by a relative error of at most 0.009.
Values may be sent and summed in bfloat16 or wider, within the bound.
A program may use at most 128 MiB of HBM per device.

v0:
```python
import jax
import jax.numpy as jnp
from jax import lax
from jax.sharding import PartitionSpec as P


def owner_tables(req_owner, req_slot, own_index, peer_count, slot_count, request_count):
    owners_all = req_owner[:, 0].reshape(peer_count, request_count)
    slots_all = req_slot.reshape(peer_count, request_count)
    mine = owners_all == own_index
    ranks = jnp.cumsum(mine.astype(jnp.int32), axis=1) - 1
    slot_ids = jnp.arange(slot_count, dtype=jnp.int32)
    chosen = mine[:, None, :] & (ranks[:, None, :] == slot_ids[None, :, None])
    send_index = jnp.sum(jnp.where(chosen, slots_all[:, None, :], 0), axis=2).reshape(-1)
    send_valid = jnp.any(chosen, axis=2).reshape(-1)
    own_owners = lax.dynamic_slice_in_dim(req_owner[:, 0], own_index * request_count, request_count)
    request_ids = jnp.arange(request_count, dtype=jnp.int32)
    earlier = (own_owners[:, None] == own_owners[None, :]) & (
        request_ids[None, :] < request_ids[:, None]
    )
    own_rank = jnp.sum(earlier.astype(jnp.int32), axis=1)
    receive_index = own_owners * slot_count + own_rank
    return (send_index, send_valid, receive_index)


def forward_product(left, fetched, term_left, term_fetch, unit_scale):
    left_terms = left[term_left]
    right_terms = fetched[term_fetch]
    total = jnp.einsum(
        "btik,btkj->bij", left_terms, right_terms, preferred_element_type=jnp.float32
    )
    return unit_scale * total


def left_adjoint(cot, fetched, term_left, term_fetch, unit_scale):
    right_terms = fetched[term_fetch]
    pieces = jnp.einsum("bij,btkj->btik", cot, right_terms, preferred_element_type=jnp.float32)
    total = jnp.zeros(cot.shape, jnp.float32).at[term_left].add(pieces)
    return unit_scale * total


def request_adjoint(
    first, first_cot, second, second_cot, term_left, term_fetch, request_count, unit_scale
):
    stacked_left = jnp.concatenate([first[term_left], second[term_left]], axis=2)
    stacked_cot = jnp.concatenate([first_cot, second_cot], axis=1)
    pieces = jnp.einsum(
        "btki,bkj->btij", stacked_left, stacked_cot, preferred_element_type=jnp.float32
    )
    total = (
        jnp.zeros((request_count, first.shape[1], first.shape[2]), jnp.float32)
        .at[term_fetch]
        .add(pieces)
    )
    return (unit_scale * total).astype(jnp.bfloat16)


def body(density_guess, cotangent, term_left, term_fetch, req_owner, req_slot):
    peer_count = lax.axis_size("row")
    own_index = lax.axis_index("row")
    request_count = req_owner.shape[0] // peer_count
    slot_count = max(2, 2 * request_count // peer_count)
    block_width = density_guess.shape[1]
    term_count = term_left.shape[1]
    unit_scale = float(block_width * term_count) ** (-0.5)
    send_index, send_valid, receive_index = owner_tables(
        req_owner, req_slot, own_index, peer_count, slot_count, request_count
    )

    def outgoing(blocks):
        return jnp.where(send_valid[:, None, None], blocks[send_index], jnp.zeros((), blocks.dtype))

    def fetch(blocks):
        return lax.all_to_all(outgoing(blocks), "row", split_axis=0, concat_axis=0, tiled=True)[
            receive_index
        ]

    def purify(density):
        fetched = fetch(density)
        square = forward_product(density, fetched, term_left, term_fetch, unit_scale).astype(
            jnp.bfloat16
        )
        cube = forward_product(square, fetched, term_left, term_fetch, unit_scale)
        fresh = (3.0 * square.astype(jnp.float32) - 2.0 * cube).astype(jnp.bfloat16)
        return (fresh, square, fetched)

    def reverse(density, square, fetched, cot):
        cube_cot = (-2.0 * cot.astype(jnp.float32)).astype(jnp.bfloat16)
        square_cot = (
            3.0 * cot.astype(jnp.float32)
            + left_adjoint(cube_cot, fetched, term_left, term_fetch, unit_scale)
        ).astype(jnp.bfloat16)
        requests = request_adjoint(
            square, cube_cot, density, square_cot, term_left, term_fetch, request_count, unit_scale
        )
        sendback = (
            jnp.zeros((peer_count * slot_count, block_width, block_width), jnp.bfloat16)
            .at[receive_index]
            .set(requests)
        )
        returned = lax.all_to_all(sendback, "row", split_axis=0, concat_axis=0, tiled=True)
        returned = jnp.where(send_valid[:, None, None], returned.astype(jnp.float32), 0.0)
        collected = jnp.zeros(density.shape, jnp.float32).at[send_index].add(returned)
        return left_adjoint(square_cot, fetched, term_left, term_fetch, unit_scale) + collected

    first, first_square, first_fetched = purify(density_guess)
    second, second_square, second_fetched = purify(first)
    first_cot = reverse(first, second_square, second_fetched, cotangent).astype(jnp.bfloat16)
    guess_grad = reverse(density_guess, first_square, first_fetched, first_cot)
    return (second, guess_grad)


def solution(mesh):
    placed = (
        P(("groups", "row"), None, None),
        P(("groups", "row"), None, None),
        P(("groups", "row"), None),
        P(("groups", "row"), None),
        P("groups", None),
        P("groups"),
    )
    return jax.shard_map(
        body,
        mesh=mesh,
        in_specs=placed,
        out_specs=(P(("groups", "row"), None, None), P(("groups", "row"), None, None)),
        check_vma=False,
    )
```

profile of v0, /device:TPU:15, one launch (start us, length us, event | category | flops | bytes accessed | tf_op | source)
XLA Modules:
  0.0 362.0 jit_solution(16952870552484408141)
XLA Ops:
  5.6 6.7 %all-to-all-start = ((bf16[64,128,128]{2,1,0:T(8,128)(2,1)}), bf16[64,128,128]{2,1,0:T(8,128)(2,1)}, u32[]{:S(2)}, u32[]{:S(2)}) async-start(bf16[64,128,128]{2,1,0:T(8,128)(2,1)} %broadcast_select_fusion.1), calls=%async_computation | async-start | bytes 4194304 | tf_op jit(solution)/shard_map/all_to_all | solution.py:74
  15.2 44.6 %all-to-all-done = bf16[64,128,128]{2,1,0:T(8,128)(2,1)} async-done(((bf16[64,128,128]{2,1,0:T(8,128)(2,1)}), bf16[64,128,128]{2,1,0:T(8,128)(2,1)}, u32[]{:S(2)}, u32[]{:S(2)}) %all-to-all-start) | async-done | bytes 2097184 | tf_op jit(solution)/shard_map/all_to_all | solution.py:74
  73.2 4.9 %all-to-all-start.1 = ((bf16[64,128,128]{2,1,0:T(8,128)(2,1)}), bf16[64,128,128]{2,1,0:T(8,128)(2,1)}, u32[]{:S(2)}, u32[]{:S(2)}) async-start(bf16[64,128,128]{2,1,0:T(8,128)(2,1)} %broadcast_select_fusion), calls=%async_computation.1 | async-start | bytes 4194304 | tf_op jit(solution)/shard_map/all_to_all | solution.py:74
  81.7 43.9 %all-to-all-done.1 = bf16[64,128,128]{2,1,0:T(8,128)(2,1)} async-done(((bf16[64,128,128]{2,1,0:T(8,128)(2,1)}), bf16[64,128,128]{2,1,0:T(8,128)(2,1)}, u32[]{:S(2)}, u32[]{:S(2)}) %all-to-all-start.1) | async-done | bytes 2097184 | tf_op jit(solution)/shard_map/all_to_all | solution.py:74
  125.6 3.2 gather_fusion.7
  131.1 3.9 %fusion.15 = bf16[16,128,128]{2,1,0:T(8,128)(2,1)} fusion(bf16[16,4,128,128]{3,2,1,0:T(8,128)(2,1)} %bitcast.115, bf16[16,4,128,128]{3,2,1,0:T(8,128)(2,1)S(1)} %bitcast.109), kind=kOutput, calls=%fused_computation.53 | convolution fusion | flops 268959744 | bytes 4718592 | tf_op jit(solution)/shard_map/btik,btkj->bij/dot_general | solution.py:29
  137.6 5.3 %copy.36 = f32[16,4,128,128]{3,2,1,0:T(8,128)} copy(f32[16,4,128,128]{2,3,1,0:T(8,128)} %convolution_bitcast_fusion.3) | data formatting | bytes 8388608 | tf_op jit(solution)/shard_map/bij,btkj->btik/transpose | solution.py:37
  143.0 8.8 %scatter_fusion = f32[16,128,128]{2,1,0:T(8,128)S(1)} fusion(f32[16,128,128]{2,1,0:T(8,128)S(1)} %broadcast.87.clone.2, s32[64]{0:T(128)S(1)} %reshape.64, f32[64,128,128]{2,1,0:T(8,128)} %bitcast.117), kind=kCustom, calls=%fused_computation.10 | custom fusion | flops 1048576 | bytes 12583168 | tf_op jit(solution)/shard_map/scatter-add | solution.py:38
  157.4 4.0 %copy.38 = bf16[16,4,128,128]{2,3,1,0:T(8,128)(2,1)} copy(bf16[16,4,128,128]{3,2,1,0:T(8,128)(2,1)} %bitcast.120) | data formatting | bytes 4194304 | tf_op jit(solution)/shard_map/gather | solution.py:27
  161.4 5.4 %fusion = f32[16,4,128,128]{3,2,1,0:T(8,128)} fusion(bf16[16,4,128,128]{2,3,1,0:T(8,128)(2,1)} %copy.39, bf16[16,4,128,128]{2,3,1,0:T(8,128)(2,1)} %copy.38, bf16[16,128,128]{2,1,0:T(8,128)(2,1)S(1)} %copy-done.14, bf16[16,128,128]{2,1,0:T(8,128)(2,1)S(1)} %copy-done.18), kind=kOutput, calls=%fused_computation.20 | convolution fusion | flops 547356672 | bytes 9437184 | tf_op jit(solution)/shard_map/btki,bkj->btij/dot_general | solution.py:47
  168.4 13.4 %scatter_fusion.2 = f32[32,128,128]{2,1,0:T(8,128)} fusion(f32[32,128,128]{2,1,0:T(8,128)} %broadcast.89.clone, s32[64]{0:T(128)S(1)} %reshape.88, f32[64,128,128]{2,1,0:T(8,128)} %bitcast.125), kind=kCustom, calls=%fused_computation.12 | custom fusion | flops 1048576 | bytes 12583168 | tf_op jit(solution)/shard_map/scatter-add | solution.py:53
  185.5 4.6 %scatter_fusion.3 = bf16[64,128,128]{2,1,0:T(8,128)(2,1)} fusion(bf16[64,128,128]{2,1,0:T(8,128)(2,1)} %broadcast_in_dim.56.clone, s32[32]{0:T(128)S(1)} %fusion.36, bf16[32,128,128]{2,1,0:T(8,128)(2,1)S(1)} %multiply_convert_fusion.1), kind=kCustom, calls=%fused_computation.13 | custom fusion | bytes 3145856 | tf_op jit(solution)/shard_map/scatter | solution.py:99
  190.2 5.0 %all-to-all-start.2 = ((bf16[64,128,128]{2,1,0:T(8,128)(2,1)}), bf16[64,128,128]{2,1,0:T(8,128)(2,1)}, u32[]{:S(2)}, u32[]{:S(2)}) async-start(bf16[64,128,128]{2,1,0:T(8,128)(2,1)} %scatter_fusion.3), calls=%async_computation.2 | async-start | bytes 4194304 | tf_op jit(solution)/shard_map/all_to_all | solution.py:101
  195.1 4.1 %copy.31 = bf16[64,128,128]{1,2,0:T(8,128)(2,1)} copy(bf16[64,128,128]{2,1,0:T(8,128)(2,1)} %gather_fusion) | data formatting | bytes 4194304 | tf_op jit(solution)/shard_map/gather | solution.py:27
  199.2 4.0 %copy.42 = bf16[16,4,128,128]{2,3,1,0:T(8,128)(2,1)} copy(bf16[16,4,128,128]{3,2,1,0:T(8,128)(2,1)} %bitcast.123) | data formatting | bytes 4194304 | tf_op jit(solution)/shard_map/gather | solution.py:27
  205.8 5.3 %copy.37 = f32[16,4,128,128]{3,2,1,0:T(8,128)} copy(f32[16,4,128,128]{2,3,1,0:T(8,128)} %convolution_bitcast_fusion.2) | data formatting | bytes 8388608 | tf_op jit(solution)/shard_map/bij,btkj->btik/transpose | solution.py:37
  211.3 8.8 %scatter_fusion.1 = f32[16,128,128]{2,1,0:T(8,128)S(1)} fusion(f32[16,128,128]{2,1,0:T(8,128)S(1)} %broadcast.87.clone.1, s32[64]{0:T(128)S(1)} %reshape.64, f32[64,128,128]{2,1,0:T(8,128)} %bitcast.118), kind=kCustom, calls=%fused_computation.11 | custom fusion | flops 1048576 | bytes 12583168 | tf_op jit(solution)/shard_map/scatter-add | solution.py:38
  220.2 22.5 %all-to-all-done.2 = bf16[64,128,128]{2,1,0:T(8,128)(2,1)} async-done(((bf16[64,128,128]{2,1,0:T(8,128)(2,1)}), bf16[64,128,128]{2,1,0:T(8,128)(2,1)}, u32[]{:S(2)}, u32[]{:S(2)}) %all-to-all-start.2) | async-done | bytes 2097184 | tf_op jit(solution)/shard_map/all_to_all | solution.py:101
  242.6 3.9 %convert_select_fusion.1 = f32[64,128,128]{2,1,0:T(8,128)} fusion(bf16[64,128,128]{2,1,0:T(8,128)(2,1)} %all-to-all-done.2, pred[64]{0:T(512)(128)(4,1)S(1)} %broadcast_in_dim.51), kind=kLoop, calls=%fused_computation.29 | loop fusion | flops 2097152 | bytes 6291520 | tf_op jit(solution)/shard_map/jit(_where)/select_n | solution.py:102
  246.5 8.9 %scatter_fusion.4 = f32[16,128,128]{2,1,0:T(8,128)S(1)} fusion(f32[16,128,128]{2,1,0:T(8,128)S(1)} %broadcast_multiply_fusion.1, s32[64]{0:T(128)S(1)} %fusion.35, f32[64,128,128]{2,1,0:T(8,128)} %convert_select_fusion.1), kind=kCustom, calls=%fused_computation.14 | custom fusion | flops 1048576 | bytes 12583168 | tf_op jit(solution)/shard_map/scatter-add | solution.py:103
  258.9 5.3 %copy.40 = f32[16,4,128,128]{3,2,1,0:T(8,128)} copy(f32[16,4,128,128]{2,3,1,0:T(8,128)} %convolution_bitcast_fusion.1) | data formatting | bytes 8388608 | tf_op jit(solution)/shard_map/bij,btkj->btik/transpose | solution.py:37
  264.4 8.8 %scatter_fusion.5 = f32[16,128,128]{2,1,0:T(8,128)S(1)} fusion(f32[16,128,128]{2,1,0:T(8,128)S(1)} %broadcast.87.clone, s32[64]{0:T(128)S(1)} %reshape.64, f32[64,128,128]{2,1,0:T(8,128)} %bitcast.119), kind=kCustom, calls=%fused_computation.15 | custom fusion | flops 1048576 | bytes 12583168 | tf_op jit(solution)/shard_map/scatter-add | solution.py:38
  275.0 4.8 %fusion.4 = f32[16,4,128,128]{3,2,1,0:T(8,128)} fusion(bf16[16,4,128,128]{2,3,1,0:T(8,128)(2,1)S(1)} %bitcast.126, bf16[16,4,128,128]{2,3,1,0:T(8,128)(2,1)} %copy.42, bf16[16,128,128]{2,1,0:T(8,128)(2,1)S(1)} %fusion.22, bf16[16,128,128]{2,1,0:T(8,128)(2,1)S(1)} %copy-done.17), kind=kOutput, calls=%fused_computation.24 | convolution fusion | flops 547356672 | bytes 9437184 | tf_op jit(solution)/shard_map/btki,bkj->btij/dot_general | solution.py:47
  280.1 8.8 %scatter_fusion.7 = f32[32,128,128]{2,1,0:T(8,128)S(1)} fusion(f32[32,128,128]{2,1,0:T(8,128)S(1)} %broadcast.89, s32[64]{0:T(128)S(1)} %reshape.88, f32[64,128,128]{2,1,0:T(8,128)} %bitcast.124), kind=kCustom, calls=%fused_computation.17 | custom fusion | flops 1048576 | bytes 12583168 | tf_op jit(solution)/shard_map/scatter-add | solution.py:53
  291.0 4.6 %scatter_fusion.8 = bf16[64,128,128]{2,1,0:T(8,128)(2,1)} fusion(bf16[64,128,128]{2,1,0:T(8,128)(2,1)} %broadcast_in_dim.56, s32[32]{0:T(128)S(1)} %fusion.36, bf16[32,128,128]{2,1,0:T(8,128)(2,1)S(1)} %multiply_convert_fusion), kind=kCustom, calls=%fused_computation.18 | custom fusion | bytes 3145856 | tf_op jit(solution)/shard_map/scatter | solution.py:99
  295.6 5.2 %all-to-all-start.3 = ((bf16[64,128,128]{2,1,0:T(8,128)(2,1)}), bf16[64,128,128]{2,1,0:T(8,128)(2,1)}, u32[]{:S(2)}, u32[]{:S(2)}) async-start(bf16[64,128,128]{2,1,0:T(8,128)(2,1)} %scatter_fusion.8), calls=%async_computation.3 | async-start | bytes 4194304 | tf_op jit(solution)/shard_map/all_to_all | solution.py:101
  300.9 3.2 fusion.14
  306.7 5.3 %copy.41 = f32[16,4,128,128]{3,2,1,0:T(8,128)} copy(f32[16,4,128,128]{2,3,1,0:T(8,128)} %convolution_bitcast_fusion) | data formatting | bytes 8388608 | tf_op jit(solution)/shard_map/bij,btkj->btik/transpose | solution.py:37
  312.2 8.8 %scatter_fusion.6 = f32[16,128,128]{2,1,0:T(8,128)S(1)} fusion(f32[16,128,128]{2,1,0:T(8,128)S(1)} %broadcast.87, s32[64]{0:T(128)S(1)} %reshape.64, f32[64,128,128]{2,1,0:T(8,128)} %bitcast.116), kind=kCustom, calls=%fused_computation.16 | custom fusion | flops 1048576 | bytes 12583168 | tf_op jit(solution)/shard_map/scatter-add | solution.py:38
  321.1 27.2 %all-to-all-done.3 = bf16[64,128,128]{2,1,0:T(8,128)(2,1)} async-done(((bf16[64,128,128]{2,1,0:T(8,128)(2,1)}), bf16[64,128,128]{2,1,0:T(8,128)(2,1)}, u32[]{:S(2)}, u32[]{:S(2)}) %all-to-all-start.3) | async-done | bytes 2097184 | tf_op jit(solution)/shard_map/all_to_all | solution.py:101
  348.3 3.9 %convert_select_fusion = f32[64,128,128]{2,1,0:T(8,128)} fusion(bf16[64,128,128]{2,1,0:T(8,128)(2,1)} %all-to-all-done.3, pred[64]{0:T(512)(128)(4,1)S(1)} %broadcast_in_dim.51), kind=kLoop, calls=%fused_computation.28 | loop fusion | flops 2097152 | bytes 6291520 | tf_op jit(solution)/shard_map/jit(_where)/select_n | solution.py:102
  352.2 8.8 %scatter_fusion.9 = f32[16,128,128]{2,1,0:T(8,128)S(1)} fusion(f32[16,128,128]{2,1,0:T(8,128)S(1)} %broadcast_multiply_fusion, s32[64]{0:T(128)S(1)} %fusion.35, f32[64,128,128]{2,1,0:T(8,128)} %convert_select_fusion), kind=kCustom, calls=%fused_computation.19 | custom fusion | flops 1048576 | bytes 12583168 | tf_op jit(solution)/shard_map/scatter-add | solution.py:103
  (103 shorter events, 55.0 us)
Async XLA Ops:
  0.6 2.5 copy-start
  5.6 6.7 %copy-start.20 = (s32[16,4]{0,1:T(4,128)S(1)}, s32[16,4]{0,1:T(4,128)}, u32[]{:S(2)}) copy-start(s32[16,4]{0,1:T(4,128)} %param.9) | copy-start | bytes 772
  5.6 6.9 %copy-start.21 = (s32[16,4]{0,1:T(4,128)S(1)}, s32[16,4]{0,1:T(4,128)}, u32[]{:S(2)}) copy-start(s32[16,4]{0,1:T(4,128)} %param.8) | copy-start | bytes 772
  5.6 54.2 %all-to-all-start = ((bf16[64,128,128]{2,1,0:T(8,128)(2,1)}), bf16[64,128,128]{2,1,0:T(8,128)(2,1)}, u32[]{:S(2)}, u32[]{:S(2)}) async-start(bf16[64,128,128]{2,1,0:T(8,128)(2,1)} %broadcast_select_fusion.1), calls=%async_computation | async-start | bytes 4194304 | tf_op jit(solution)/shard_map/all_to_all | solution.py:74
  12.7 2.2 copy-start.19
  63.2 5.2 %copy-start.2 = (bf16[64,128,128]{2,1,0:T(8,128)(2,1)}, bf16[64,128,128]{2,1,0:T(8,128)(2,1)S(1)}, u32[]{:S(2)}) copy-start(bf16[64,128,128]{2,1,0:T(8,128)(2,1)S(1)} %gather_fusion.3) | copy-start | bytes 6291460
  73.2 52.4 %all-to-all-start.1 = ((bf16[64,128,128]{2,1,0:T(8,128)(2,1)}), bf16[64,128,128]{2,1,0:T(8,128)(2,1)}, u32[]{:S(2)}, u32[]{:S(2)}) async-start(bf16[64,128,128]{2,1,0:T(8,128)(2,1)} %broadcast_select_fusion), calls=%async_computation.1 | async-start | bytes 4194304 | tf_op jit(solution)/shard_map/all_to_all | solution.py:74
  79.1 46.6 %copy-start.8 = (bf16[64,128,128]{2,1,0:T(8,128)(2,1)}, bf16[64,128,128]{2,1,0:T(8,128)(2,1)S(1)}, u32[]{:S(2)}) copy-start(bf16[64,128,128]{2,1,0:T(8,128)(2,1)S(1)} %gather_fusion.5) | copy-start | bytes 6291460
  131.1 72.1 %copy-start.5 = (bf16[64,128,128]{2,1,0:T(8,128)(2,1)}, bf16[64,128,128]{2,1,0:T(8,128)(2,1)S(1)}, u32[]{:S(2)}) copy-start(bf16[64,128,128]{2,1,0:T(8,128)(2,1)S(1)} %gather_fusion.8) | copy-start | bytes 6291460
  131.1 3.9 %copy-start.11 = (bf16[16,128,128]{2,1,0:T(8,128)(2,1)S(1)}, bf16[16,128,128]{2,1,0:T(8,128)(2,1)}, u32[]{:S(2)}) copy-start(bf16[16,128,128]{2,1,0:T(8,128)(2,1)} %param.7) | copy-start | bytes 1572868
  157.4 4.0 %copy-start.14 = (bf16[16,128,128]{2,1,0:T(8,128)(2,1)S(1)}, bf16[16,128,128]{2,1,0:T(8,128)(2,1)}, u32[]{:S(2)}) copy-start(bf16[16,128,128]{2,1,0:T(8,128)(2,1)} %get-tuple-element.3) | copy-start | bytes 1572868
  157.4 4.0 %copy-start.18 = (bf16[16,128,128]{2,1,0:T(8,128)(2,1)S(1)}, bf16[16,128,128]{2,1,0:T(8,128)(2,1)}, u32[]{:S(2)}) copy-start(bf16[16,128,128]{2,1,0:T(8,128)(2,1)} %get-tuple-element.2) | copy-start | bytes 1572868
  190.2 52.5 %all-to-all-start.2 = ((bf16[64,128,128]{2,1,0:T(8,128)(2,1)}), bf16[64,128,128]{2,1,0:T(8,128)(2,1)}, u32[]{:S(2)}, u32[]{:S(2)}) async-start(bf16[64,128,128]{2,1,0:T(8,128)(2,1)} %scatter_fusion.3), calls=%async_computation.2 | async-start | bytes 4194304 | tf_op jit(solution)/shard_map/all_to_all | solution.py:101
  199.2 4.0 %copy-start.15 = (bf16[16,128,128]{2,1,0:T(8,128)(2,1)S(1)}, bf16[16,128,128]{2,1,0:T(8,128)(2,1)}, u32[]{:S(2)}) copy-start(bf16[16,128,128]{2,1,0:T(8,128)(2,1)} %get-tuple-element.3) | copy-start | bytes 1572868
  246.5 9.8 %copy-start.3 = (bf16[64,128,128]{2,1,0:T(8,128)(2,1)S(1)}, bf16[64,128,128]{2,1,0:T(8,128)(2,1)}, u32[]{:S(2)}) copy-start(bf16[64,128,128]{2,1,0:T(8,128)(2,1)} %copy-done.2) | copy-start | bytes 6291460
  255.5 0.8 copy-start.16
  273.2 1.8 copy-start.10
  273.2 1.9 copy-start.17
  273.4 6.5 %copy-start.12 = (bf16[16,128,128]{2,1,0:T(8,128)(2,1)}, bf16[16,128,128]{2,1,0:T(8,128)(2,1)S(1)}, u32[]{:S(2)}) copy-start(bf16[16,128,128]{2,1,0:T(8,128)(2,1)S(1)} %fusion.22) | copy-start | bytes 1572868
  295.6 5.2 %copy-start.6 = (bf16[64,128,128]{2,1,0:T(8,128)(2,1)S(1)}, bf16[64,128,128]{2,1,0:T(8,128)(2,1)}, u32[]{:S(2)}) copy-start(bf16[64,128,128]{2,1,0:T(8,128)(2,1)} %copy-done.5) | copy-start | bytes 6291460
  295.6 5.2 %copy-start.9 = (bf16[16,128,128]{2,1,0:T(8,128)(2,1)S(1)}, bf16[16,128,128]{2,1,0:T(8,128)(2,1)}, u32[]{:S(2)}) copy-start(bf16[16,128,128]{2,1,0:T(8,128)(2,1)} %fusion.15) | copy-start | bytes 1572868
  295.6 52.7 %all-to-all-start.3 = ((bf16[64,128,128]{2,1,0:T(8,128)(2,1)}), bf16[64,128,128]{2,1,0:T(8,128)(2,1)}, u32[]{:S(2)}, u32[]{:S(2)}) async-start(bf16[64,128,128]{2,1,0:T(8,128)(2,1)} %scatter_fusion.8), calls=%async_computation.3 | async-start | bytes 4194304 | tf_op jit(solution)/shard_map/all_to_all | solution.py:101
  300.8 3.3 copy-start.4
  300.8 3.3 copy-start.13
  352.2 9.8 %copy-start.1 = (bf16[16,128,128]{2,1,0:T(8,128)(2,1)S(1)}, bf16[16,128,128]{2,1,0:T(8,128)(2,1)}, u32[]{:S(2)}) copy-start(bf16[16,128,128]{2,1,0:T(8,128)(2,1)} %param.6) | copy-start | bytes 1572868
  361.0 1.0 copy-start.7
where the time goes:
time: 365 us; the launch traced here: 362 us
  waiting for transfers between devices  138 us (38%)
  other arithmetic  92.4 us (25%)
  local copies, waits for them, and re-layouts  75.4 us (21%)
  matrix products  33.2 us (9%)
  starting transfers between devices  21.7 us (6%)
    all_to_all x2, waiting for transfers between devices, fetch(): lax.all_to_all(outgoing(blocks), 'row', split_axis=0, concat_axis=0, tile...  88.5 us
    all_to_all x2, waiting for transfers between devices, reverse(): lax.all_to_all(sendback, 'row', split_axis=0, concat_axis=0, tiled=True)  49.7 us
    scatter-add x4, other arithmetic, left_adjoint(): total = jnp.zeros(cot.shape, jnp.float32).at[term_left].add(pieces)  35.2 us
    gather x8, local copies, waits for them, and re-layouts, forward_product(): left_terms = left[term_left]  23.2 us
    scatter-add x2, other arithmetic, request_adjoint(): total = jnp.zeros((request_count, first.shape[1], first.shape[2]), jnp.fl...  22.2 us
    transpose x4, local copies, waits for them, and re-layouts, left_adjoint(): jnp.einsum('bij,btkj->btik', cot, right_terms, preferred_element_type=jnp...  21.4 us
    scatter-add x2, other arithmetic, reverse(): jnp.zeros(density.shape, jnp.float32).at[send_index].add(returned)  17.6 us
    dot_general x4, matrix products, forward_product(): jnp.einsum('btik,btkj->bij', left_terms, right_terms, preferred_element_t...  12.4 us
  transfers between devices with their start and end apart: 4, of which 4 were waited for; matrix products, arithmetic and copies ran while one was open for 14% of the time, Pallas kernels for 0%

commit v1 on v0

v1 whole, which is shorter than its diff:
```python
import functools

import jax
import jax.numpy as jnp
from jax import lax
from jax.experimental import pallas as pl
from jax.experimental.pallas import tpu as pltpu
from jax.sharding import PartitionSpec as P

F32 = jnp.float32
BF16 = jnp.bfloat16
VMEM_LIMIT = 56 * 1024 * 1024


def owner_tables(req_owner, req_slot, own_index, peer_count, slot_count, request_count):
    owners_all = req_owner[:, 0].reshape(peer_count, request_count)
    slots_all = req_slot.reshape(peer_count, request_count)
    mine = owners_all == own_index
    ranks = jnp.cumsum(mine.astype(jnp.int32), axis=1) - 1
    slot_ids = jnp.arange(slot_count, dtype=jnp.int32)
    chosen = mine[:, None, :] & (ranks[:, None, :] == slot_ids[None, :, None])
    send_index = jnp.sum(jnp.where(chosen, slots_all[:, None, :], 0), axis=2).reshape(-1)
    send_valid = jnp.any(chosen, axis=2).reshape(-1)
    own_owners = lax.dynamic_slice_in_dim(req_owner[:, 0], own_index * request_count, request_count)
    request_ids = jnp.arange(request_count, dtype=jnp.int32)
    earlier = (own_owners[:, None] == own_owners[None, :]) & (
        request_ids[None, :] < request_ids[:, None]
    )
    own_rank = jnp.sum(earlier.astype(jnp.int32), axis=1)
    receive_index = own_owners * slot_count + own_rank
    return (send_index, send_valid.astype(jnp.int32), receive_index)


def dot(a, b):
    return jnp.dot(a, b, preferred_element_type=F32)


def dot_rt(a, b):
    return lax.dot_general(a, b, (((1,), (1,)), ((), ())), preferred_element_type=F32)


def forward_sums(left, right, tl, tr, b, terms):
    lhs = jnp.concatenate([left[tl[b * terms + t]] for t in range(terms)], axis=1)
    rhs = jnp.concatenate([right[tr[b * terms + t]] for t in range(terms)], axis=0)
    return dot(lhs, rhs)


def left_adjoint(cots, right, tl, tr, acc, terms):
    acc[...] = jnp.zeros_like(acc)

    @pl.loop(0, cots.shape[0], unroll=2)
    def _(b):
        rhs = jnp.concatenate([right[tr[b * terms + t]] for t in range(terms)], axis=0)
        piece = dot_rt(cots[b], rhs)
        width = cots.shape[2]
        for t in range(terms):
            acc[tl[b * terms + t]] += piece[:, t * width:(t + 1) * width]


def gather_kernel(index, blocks, out):
    @pl.loop(0, out.shape[0], unroll=4)
    def _(s):
        out[s] = blocks[index[s]]


def forward_kernel(terms, scale, tl, tr, index, dens, right, fresh, square, *out):
    blocks = dens.shape[0]

    @pl.loop(0, blocks, unroll=4)
    def _(b):
        square[b] = (scale * forward_sums(dens, right, tl, tr, b, terms)).astype(BF16)

    @pl.loop(0, blocks, unroll=4)
    def _(b):
        cube = scale * forward_sums(square, right, tl, tr, b, terms)
        fresh[b] = (3.0 * square[b].astype(F32) - 2.0 * cube).astype(BF16)

    if out:
        gather_kernel(index, fresh, out[0])


def cot_phase(terms, scale, tl, tr, tf, rix, dens, square, right, cot, sqcot, sendback, acc, cube, both, racc):
    blocks, width = dens.shape[0], dens.shape[2]

    @pl.loop(0, blocks, unroll=4)
    def _(b):
        cube[b] = (-2.0 * cot[b].astype(F32)).astype(BF16)
        both[b] = jnp.concatenate([square[b].T, dens[b].T], axis=1)

    left_adjoint(cube, right, tl, tr, acc, terms)

    @pl.loop(0, blocks, unroll=4)
    def _(b):
        sqcot[b] = (3.0 * cot[b].astype(F32) + scale * acc[b]).astype(BF16)

    racc[...] = jnp.zeros_like(racc)

    @pl.loop(0, blocks, unroll=2)
    def _(b):
        lhs = jnp.concatenate([both[tl[b * terms + t]] for t in range(terms)], axis=0)
        rhs = jnp.concatenate([cube[b], sqcot[b]], axis=0)
        piece = dot(lhs, rhs)
        for t in range(terms):
            racc[tf[b * terms + t]] += piece[t * width:(t + 1) * width]

    @pl.loop(0, sendback.shape[0], unroll=4)
    def _(s):
        sendback[s] = jnp.zeros(sendback.shape[1:], BF16)

    @pl.loop(0, racc.shape[0], unroll=4)
    def _(q):
        sendback[rix[q]] = (scale * racc[q]).astype(BF16)


def reverse_kernel(terms, scale, tl, tr, tf, rix, dens, square, right, cot, sqcot, sendback, acc, cube, both, racc):
    cot_phase(terms, scale, tl, tr, tf, rix, dens, square, right, cot, sqcot, sendback, acc, cube, both, racc)


def collect(index, valid, returned, grad):
    @pl.loop(0, returned.shape[0])
    def _(s):
        @pl.when(valid[s] > 0)
        def _():
            grad[index[s]] += returned[s].astype(F32)


def chained_kernel(terms, scale, tl, tr, tf, rix, index, valid, dens, square, right, local, returned, sqcot, sendback, acc, cube, both, racc, cot):
    acc[...] = local[...]
    collect(index, valid, returned, acc)
    cot[...] = acc[...].astype(BF16)
    cot_phase(terms, scale, tl, tr, tf, rix, dens, square, right, cot, sqcot, sendback, acc, cube, both, racc)


def local_kernel(terms, scale, tl, tr, sqcot, right, grad):
    left_adjoint(sqcot, right, tl, tr, grad, terms)
    grad[...] = scale * grad[...]


def final_kernel(index, valid, local, returned, grad):
    grad[...] = local[...]
    collect(index, valid, returned, grad)


def call(kernel, prefetch, arrays, outs, scratch=(), flops=0):
    whole = pl.BlockSpec(memory_space=pltpu.VMEM)
    smem = pl.BlockSpec(memory_space=pltpu.SMEM)
    moved = sum(a.size * a.dtype.itemsize for a in arrays)
    return pl.pallas_call(
        kernel,
        out_shape=outs,
        in_specs=[smem] * len(prefetch) + [whole] * len(arrays),
        out_specs=[whole] * len(outs),
        scratch_shapes=list(scratch),
        cost_estimate=pl.CostEstimate(flops=flops, bytes_accessed=moved, transcendentals=0),
        compiler_params=pltpu.CompilerParams(vmem_limit_bytes=VMEM_LIMIT),
    )(*prefetch, *arrays)


def body(density_guess, cotangent, term_left, term_fetch, req_owner, req_slot):
    peer_count = lax.axis_size("row")
    own_index = lax.axis_index("row")
    request_count = req_owner.shape[0] // peer_count
    slot_count = max(2, 2 * request_count // peer_count)
    blocks, width = density_guess.shape[0], density_guess.shape[1]
    terms = term_left.shape[1]
    scale = float(width * terms) ** (-0.5)
    send_index, send_valid, receive_index = owner_tables(
        req_owner, req_slot, own_index, peer_count, slot_count, request_count
    )
    slots = peer_count * slot_count
    tl = term_left.reshape(-1)
    tf = term_fetch.reshape(-1)
    tr = receive_index[tf]

    def shape(n, dtype):
        return jax.ShapeDtypeStruct((n, width, width), dtype)

    def exchange(x):
        return lax.all_to_all(x, "row", split_axis=0, concat_axis=0, tiled=True)

    work = 2 * blocks * terms * width ** 3
    common = [
        pltpu.VMEM((blocks, width, width), F32),
        pltpu.VMEM((blocks, width, width), BF16),
        pltpu.VMEM((blocks, width, 2 * width), BF16),
        pltpu.VMEM((request_count, width, width), F32),
    ]
    forward = functools.partial(forward_kernel, terms, scale)
    (out0,) = call(gather_kernel, [send_index], [density_guess], [shape(slots, BF16)])
    right0 = exchange(out0)
    first, square1, out1 = call(
        forward, [tl, tr, send_index], [density_guess, right0],
        [shape(blocks, BF16), shape(blocks, BF16), shape(slots, BF16)], flops=2 * work)
    right1 = exchange(out1)
    second, square2 = call(
        forward, [tl, tr, send_index], [first, right1],
        [shape(blocks, BF16), shape(blocks, BF16)], flops=2 * work)
    sqcot2, back2 = call(
        functools.partial(reverse_kernel, terms, scale), [tl, tr, tf, receive_index],
        [first, square2, right1, cotangent],
        [shape(blocks, BF16), shape(slots, BF16)], common, flops=3 * work)
    returned2 = exchange(back2)
    local = functools.partial(local_kernel, terms, scale)
    (local2,) = call(local, [tl, tr], [sqcot2, right1], [shape(blocks, F32)], flops=work)
    sqcot1, back1 = call(
        functools.partial(chained_kernel, terms, scale),
        [tl, tr, tf, receive_index, send_index, send_valid],
        [density_guess, square1, right0, local2, returned2],
        [shape(blocks, BF16), shape(slots, BF16)],
        common + [pltpu.VMEM((blocks, width, width), BF16)], flops=3 * work)
    returned1 = exchange(back1)
    (local1,) = call(local, [tl, tr], [sqcot1, right0], [shape(blocks, F32)], flops=work)
    (grad,) = call(final_kernel, [send_index, send_valid], [local1, returned1], [shape(blocks, F32)])
    return (second, grad)


def solution(mesh):
    placed = (
        P(("groups", "row"), None, None),
        P(("groups", "row"), None, None),
        P(("groups", "row"), None),
        P(("groups", "row"), None),
        P("groups", None),
        P("groups"),
    )
    return jax.shard_map(
        body,
        mesh=mesh,
        in_specs=placed,
        out_specs=(P(("groups", "row"), None, None), P(("groups", "row"), None, None)),
        check_vma=False,
    )
```

time: 365 us -> 259 us (0.71)
  other arithmetic: 92.4 us -> 1.46 us
  local copies, waits for them, and re-layouts: 75.4 us -> 10.5 us
  Pallas kernels: 0 us -> 48.3 us
  waiting for transfers between devices: 138 us -> 176 us
  matrix products: 33.2 us -> 0 us
    scatter-add x8 -> x0, other arithmetic: 75.1 us -> none  [the longest x4 35.2 us: left_adjoint(): total = jnp.zeros(cot.shape, jnp.float32).at[term_left].add(pieces)]
    pallas_call x0 -> x8, Pallas kernels: none -> 48.3 us  [call(): pl.pallas_call(kernel, out_shape=outs, in_specs=[smem] * len(prefetch) +...]
    all_to_all x4, waiting for transfers between devices: 138 us -> 176 us  [exchange(): return lax.all_to_all(x, 'row', split_axis=0, concat_axis=0, tiled=True)]
    dot_general x10 -> x0, matrix products: 33.2 us -> none  [the longest x4 12.4 us: forward_product(): jnp.einsum('btik,btkj->bij', left_terms, right_terms, preferred_element_t...]
    gather x14 -> x1, local copies, waits for them, and re-layouts: 33.8 us -> 1.26 us  [body(): tr = receive_index[tf]]
    transpose x4 -> x0, local copies, waits for them, and re-layouts: 21.4 us -> none  [left_adjoint(): jnp.einsum('bij,btkj->btik', cot, right_terms, preferred_element_type=jnp...]
    select_n x8 -> x1, other arithmetic: 10.9 us -> 0.01 us  [body(): tr = receive_index[tf]]
    scatter x2 -> x0, local copies, waits for them, and re-layouts: 9.18 us -> none  [reverse(): sendback = jnp.zeros((peer_count * slot_count, block_width, block_width),...]
  transfers between devices with their start and end apart: 4 -> 4, of which waited for: 4 -> 4; matrix products, arithmetic and copies ran while one was open for 14% -> 2% of each run, Pallas kernels for 0% -> 4%
where the time goes in v1:
time: 259 us; the launch traced here: 258 us
  waiting for transfers between devices  176 us (68%)
  Pallas kernels  48.3 us (19%)
  starting transfers between devices  21.3 us (8%)
  local copies, waits for them, and re-layouts  10.5 us (4%)
    all_to_all x4, waiting for transfers between devices, exchange(): return lax.all_to_all(x, 'row', split_axis=0, concat_axis=0, tiled=True)  176 us
    pallas_call x8, Pallas kernels, call(): pl.pallas_call(kernel, out_shape=outs, in_specs=[smem] * len(prefetch) +...  48.3 us
    all_to_all x4, starting transfers between devices, exchange(): return lax.all_to_all(x, 'row', split_axis=0, concat_axis=0, tiled=True)  21.3 us
    unnamed x18, local copies, waits for them, and re-layouts  5.48 us
  transfers between devices with their start and end apart: 4, of which 4 were waited for; matrix products, arithmetic and copies ran while one was open for 2% of the time, Pallas kernels for 4%

profile of v1, /device:TPU:15, one launch (start us, length us, event | category | flops | bytes accessed | tf_op | source)
XLA Modules:
  0.0 258.1 jit_solution(5188572683121319621)
XLA Ops:
  0.6 0.7 compare_reduce_fusion
  1.3 0.1 eq.48
  1.4 0.2 reduce_window_sum.11
  1.6 0.8 broadcast_in_dim.14
  2.4 0.1 select_reduce_fusion
  2.6 0.7 reshape.72.index
  3.3 2.6 %shard_map.77 = bf16[64,128,128]{2,1,0:T(8,128)(2,1)} custom-call(s32[64]{0:T(128)} %reshape.72.index, bf16[16,128,128]{2,1,0:T(8,128)(2,1)} %dens.3), custom_call_target="tpu_custom_call" | custom-call | bytes 524288 | tf_op jit(solution)/shard_map/pallas_call | solution.py:148
  5.9 6.7 %all-to-all-start = ((bf16[64,128,128]{2,1,0:T(8,128)(2,1)}), bf16[64,128,128]{2,1,0:T(8,128)(2,1)S(1)}, u32[]{:S(2)}, u32[]{:S(2)}) async-start(bf16[64,128,128]{2,1,0:T(8,128)(2,1)} %shard_map.77), calls=%async_computation | async-start | bytes 4194304 | tf_op jit(solution)/shard_map/all_to_all | solution.py:179
  12.9 0.7 reshape.70.tl
  13.6 0.2 convert_reduce_fusion
  13.9 1.3 gather_fusion
  15.2 44.9 %all-to-all-done.right = bf16[64,128,128]{2,1,0:T(8,128)(2,1)S(1)} async-done(((bf16[64,128,128]{2,1,0:T(8,128)(2,1)}), bf16[64,128,128]{2,1,0:T(8,128)(2,1)S(1)}, u32[]{:S(2)}, u32[]{:S(2)}) %all-to-all-start) | async-done | bytes 2097184 | tf_op jit(solution)/shard_map/all_to_all | solution.py:179
  60.0 1.3 copy-done.1
  61.4 6.0 %shard_map.78 = (bf16[16,128,128]{2,1,0:T(8,128)(2,1)}, bf16[16,128,128]{2,1,0:T(8,128)(2,1)}, bf16[64,128,128]{2,1,0:T(8,128)(2,1)}) custom-call(s32[64]{0:T(128)} %reshape.70.tl, s32[64]{0:T(128)} %gather_fusion, s32[64]{0:T(128)} %reshape.72.index, bf16[16,128,128]{2,1,0:T(8,128)(2,1)} %dens.3, bf16[64,128,128]{2,1,0:T(8,128)(2,1)} %copy-done.1), custom_call_target="tpu_custom_call" | custom-call | flops 536870912 | bytes 2621440 | tf_op jit(solution)/shard_map/pallas_call | solution.py:148
  67.3 4.9 %all-to-all-start.1 = ((bf16[64,128,128]{2,1,0:T(8,128)(2,1)}), bf16[64,128,128]{2,1,0:T(8,128)(2,1)S(1)}, u32[]{:S(2)}, u32[]{:S(2)}) async-start(bf16[64,128,128]{2,1,0:T(8,128)(2,1)} %get-tuple-element.12), calls=%async_computation.1 | async-start | bytes 4194304 | tf_op jit(solution)/shard_map/all_to_all | solution.py:179
  72.3 0.6 reshape.73.tf
  72.9 46.8 %all-to-all-done.1.right = bf16[64,128,128]{2,1,0:T(8,128)(2,1)S(1)} async-done(((bf16[64,128,128]{2,1,0:T(8,128)(2,1)}), bf16[64,128,128]{2,1,0:T(8,128)(2,1)S(1)}, u32[]{:S(2)}, u32[]{:S(2)}) %all-to-all-start.1) | async-done | bytes 2097184 | tf_op jit(solution)/shard_map/all_to_all | solution.py:179
  119.7 1.3 copy-done.2
  121.0 4.9 %shard_map.79 = (bf16[16,128,128]{2,1,0:T(8,128)(2,1)}, bf16[16,128,128]{2,1,0:T(8,128)(2,1)}) custom-call(s32[64]{0:T(128)} %reshape.70.tl, s32[64]{0:T(128)} %gather_fusion, s32[64]{0:T(128)} %reshape.72.index, bf16[16,128,128]{2,1,0:T(8,128)(2,1)} %get-tuple-element.11.dens, bf16[64,128,128]{2,1,0:T(8,128)(2,1)} %copy-done.2), custom_call_target="tpu_custom_call" | custom-call | flops 536870912 | bytes 2621440 | tf_op jit(solution)/shard_map/pallas_call | solution.py:148
  125.9 9.4 %shard_map.80 = (bf16[16,128,128]{2,1,0:T(8,128)(2,1)}, bf16[64,128,128]{2,1,0:T(8,128)(2,1)}) custom-call(s32[64]{0:T(128)} %reshape.70.tl, s32[64]{0:T(128)} %gather_fusion, s32[64]{0:T(128)} %reshape.73.tf, s32[32]{0:T(128)} %copy-done, bf16[16,128,128]{2,1,0:T(8,128)(2,1)} %get-tuple-element.11.dens, bf16[16,128,128]{2,1,0:T(8,128)(2,1)} %get-tuple-element.15.square, ...), custom_call_target="tpu_custom_call" | custom-call | flops 805306368 | bytes 3670016 | tf_op jit(solution)/shard_map/pallas_call | solution.py:148
  135.3 4.9 %all-to-all-start.2 = ((bf16[64,128,128]{2,1,0:T(8,128)(2,1)}), bf16[64,128,128]{2,1,0:T(8,128)(2,1)S(1)}, u32[]{:S(2)}, u32[]{:S(2)}) async-start(bf16[64,128,128]{2,1,0:T(8,128)(2,1)} %get-tuple-element.17), calls=%async_computation.2 | async-start | bytes 4194304 | tf_op jit(solution)/shard_map/all_to_all | solution.py:179
  140.2 0.1 fusion.1
  140.4 0.6 reshape.74.valid
  141.0 4.9 %shard_map.81.local = f32[16,128,128]{2,1,0:T(8,128)} custom-call(s32[64]{0:T(128)} %reshape.70.tl, s32[64]{0:T(128)} %gather_fusion, bf16[16,128,128]{2,1,0:T(8,128)(2,1)} %get-tuple-element.16.sqcot, bf16[64,128,128]{2,1,0:T(8,128)(2,1)} %copy-done.2), custom_call_target="tpu_custom_call" | custom-call | flops 268435456 | bytes 2621440 | tf_op jit(solution)/shard_map/pallas_call | solution.py:148
  146.0 41.6 %all-to-all-done.2.returned = bf16[64,128,128]{2,1,0:T(8,128)(2,1)S(1)} async-done(((bf16[64,128,128]{2,1,0:T(8,128)(2,1)}), bf16[64,128,128]{2,1,0:T(8,128)(2,1)S(1)}, u32[]{:S(2)}, u32[]{:S(2)}) %all-to-all-start.2) | async-done | bytes 2097184 | tf_op jit(solution)/shard_map/all_to_all | solution.py:179
  187.6 1.3 copy-done.4
  188.9 11.5 %shard_map.82 = (bf16[16,128,128]{2,1,0:T(8,128)(2,1)}, bf16[64,128,128]{2,1,0:T(8,128)(2,1)}) custom-call(s32[64]{0:T(128)} %reshape.70.tl, s32[64]{0:T(128)} %gather_fusion, s32[64]{0:T(128)} %reshape.73.tf, s32[32]{0:T(128)} %copy-done, s32[64]{0:T(128)} %reshape.72.index, s32[64]{0:T(128)} %reshape.74.valid, bf16[16,128,128]{2,1,0:T(8,128)(2,1)} %dens.3, ...), custom_call_target="tpu_custom_call" | custom-call | flops 805306368 | bytes 6291456 | tf_op jit(solution)/shard_map/pallas_call | solution.py:148
  200.4 4.8 %all-to-all-start.3 = ((bf16[64,128,128]{2,1,0:T(8,128)(2,1)}), bf16[64,128,128]{2,1,0:T(8,128)(2,1)S(1)}, u32[]{:S(2)}, u32[]{:S(2)}) async-start(bf16[64,128,128]{2,1,0:T(8,128)(2,1)} %get-tuple-element.19), calls=%async_computation.3 | async-start | bytes 4194304 | tf_op jit(solution)/shard_map/all_to_all | solution.py:179
  205.2 4.9 %shard_map.83.local = f32[16,128,128]{2,1,0:T(8,128)} custom-call(s32[64]{0:T(128)} %reshape.70.tl, s32[64]{0:T(128)} %gather_fusion, bf16[16,128,128]{2,1,0:T(8,128)(2,1)} %get-tuple-element.18.sqcot, bf16[64,128,128]{2,1,0:T(8,128)(2,1)} %copy-done.1), custom_call_target="tpu_custom_call" | custom-call | flops 268435456 | bytes 2621440 | tf_op jit(solution)/shard_map/pallas_call | solution.py:148
  210.2 42.5 %all-to-all-done.3.returned = bf16[64,128,128]{2,1,0:T(8,128)(2,1)S(1)} async-done(((bf16[64,128,128]{2,1,0:T(8,128)(2,1)}), bf16[64,128,128]{2,1,0:T(8,128)(2,1)S(1)}, u32[]{:S(2)}, u32[]{:S(2)}) %all-to-all-start.3) | async-done | bytes 2097184 | tf_op jit(solution)/shard_map/all_to_all | solution.py:179
  252.7 1.3 copy-done.3
  254.0 4.1 %shard_map.84 = f32[16,128,128]{2,1,0:T(8,128)} custom-call(s32[64]{0:T(128)} %reshape.72.index, s32[64]{0:T(128)} %reshape.74.valid, f32[16,128,128]{2,1,0:T(8,128)} %shard_map.83.local, bf16[64,128,128]{2,1,0:T(8,128)(2,1)} %copy-done.3), custom_call_target="tpu_custom_call" | custom-call | bytes 3145728 | tf_op jit(solution)/shard_map/pallas_call | solution.py:148
  (24 shorter events, 0.6 us)
Async XLA Ops:
  5.9 6.7 %copy-start.6 = (s32[16,4]{0,1:T(4,128)S(1)}, s32[16,4]{0,1:T(4,128)}, u32[]{:S(2)}) copy-start(s32[16,4]{0,1:T(4,128)} %param.9) | copy-start | bytes 772
  5.9 6.9 %copy-start.7 = (s32[16,4]{0,1:T(4,128)S(1)}, s32[16,4]{0,1:T(4,128)}, u32[]{:S(2)}) copy-start(s32[16,4]{0,1:T(4,128)} %param.8) | copy-start | bytes 772
  5.9 7.6 %copy-start.5 = (s32[512,1]{0,1:T(1,128)S(1)}, s32[512,1]{0,1:T(1,128)}, u32[]{:S(2)}) copy-start(s32[512,1]{0,1:T(1,128)} %param.10) | copy-start | bytes 6148
  5.9 54.1 %all-to-all-start = ((bf16[64,128,128]{2,1,0:T(8,128)(2,1)}), bf16[64,128,128]{2,1,0:T(8,128)(2,1)S(1)}, u32[]{:S(2)}, u32[]{:S(2)}) async-start(bf16[64,128,128]{2,1,0:T(8,128)(2,1)} %shard_map.77), calls=%async_computation | async-start | bytes 4194304 | tf_op jit(solution)/shard_map/all_to_all | solution.py:179
  13.9 53.4 %copy-start = (s32[32]{0:T(128)}, s32[32]{0:T(128)S(1)}, u32[]{:S(2)}) copy-start(s32[32]{0:T(128)S(1)} %multiply_add_fusion.rix) | copy-start | bytes 388
  60.0 1.3 copy-start.1
  67.3 52.3 %all-to-all-start.1 = ((bf16[64,128,128]{2,1,0:T(8,128)(2,1)}), bf16[64,128,128]{2,1,0:T(8,128)(2,1)S(1)}, u32[]{:S(2)}, u32[]{:S(2)}) async-start(bf16[64,128,128]{2,1,0:T(8,128)(2,1)} %get-tuple-element.12), calls=%async_computation.1 | async-start | bytes 4194304 | tf_op jit(solution)/shard_map/all_to_all | solution.py:179
  119.7 1.3 copy-start.2
  135.3 52.3 %all-to-all-start.2 = ((bf16[64,128,128]{2,1,0:T(8,128)(2,1)}), bf16[64,128,128]{2,1,0:T(8,128)(2,1)S(1)}, u32[]{:S(2)}, u32[]{:S(2)}) async-start(bf16[64,128,128]{2,1,0:T(8,128)(2,1)} %get-tuple-element.17), calls=%async_computation.2 | async-start | bytes 4194304 | tf_op jit(solution)/shard_map/all_to_all | solution.py:179
  187.6 1.3 copy-start.4
  200.4 52.3 %all-to-all-start.3 = ((bf16[64,128,128]{2,1,0:T(8,128)(2,1)}), bf16[64,128,128]{2,1,0:T(8,128)(2,1)S(1)}, u32[]{:S(2)}, u32[]{:S(2)}) async-start(bf16[64,128,128]{2,1,0:T(8,128)(2,1)} %get-tuple-element.19), calls=%async_computation.3 | async-start | bytes 4194304 | tf_op jit(solution)/shard_map/all_to_all | solution.py:179
  252.7 1.3 copy-start.3

commit v2 on v1

--- a/solution.py
+++ b/solution.py
@@ -10,6 +10,7 @@
 F32 = jnp.float32
 BF16 = jnp.bfloat16
 VMEM_LIMIT = 56 * 1024 * 1024
+GATHER_BYTES = 16 * 1024 * 1024
 
 
 def owner_tables(req_owner, req_slot, own_index, peer_count, slot_count, request_count):
@@ -141,6 +142,198 @@
     collect(index, valid, returned, grad)
 
 
+def spread_kernel(nz, ny, nc, parts, own, spread, send_sem, recv_sem, own_sem):
+    me = lax.axis_index("row")
+    core, y, z = me % nc, (me // nc) % ny, me // (nc * ny)
+    count = own.shape[0]
+    size = count // parts
+    UP, DOWN, ACROSS, TWIN = 0, 1, 2, 3
+    steps = {UP: nc * ny, DOWN: -nc * ny}
+
+    def target(way):
+        if way == ACROSS:
+            return (z * ny + (ny - 1 - y)) * nc + core
+        if way == TWIN:
+            return (z * ny + y) * nc + (nc - 1 - core)
+        return me + steps[way]
+
+    def exists(way):
+        return {UP: z + 1 < nz, DOWN: z > 0}[way]
+
+    barrier = pltpu.get_barrier_semaphore()
+
+    def greet(way):
+        pl.semaphore_signal(barrier, inc=1, device_id={"row": target(way)}, device_id_type=pl.DeviceIdType.MESH)
+
+    for way in (UP, DOWN):
+        pl.when(exists(way))(functools.partial(greet, way))
+    for way in (ACROSS, TWIN):
+        greet(way)
+    pl.semaphore_wait(barrier, 2 + (z + 1 < nz).astype(jnp.int32) + (z > 0).astype(jnp.int32))
+
+    def copy(way, zz, yy, s, from_own=False):
+        origin = (zz * ny + yy) * nc + core
+        place = spread.at[pl.ds(origin * count + s * size, size)]
+        source = own.at[pl.ds(s * size, size)] if from_own else place
+        return pltpu.make_async_remote_copy(
+            src_ref=source, dst_ref=place,
+            send_sem=send_sem.at[way, zz * ny + yy, s], recv_sem=recv_sem.at[origin, s],
+            device_id={"row": target(way)}, device_id_type=pl.DeviceIdType.MESH)
+
+    def arrived(zz, yy, s, plane):
+        origin = (zz * ny + yy) * nc + plane
+        place = spread.at[pl.ds(origin * count + s * size, size)]
+        pltpu.make_async_remote_copy(
+            src_ref=place, dst_ref=place,
+            send_sem=send_sem.at[TWIN, 0, 0], recv_sem=recv_sem.at[origin, s],
+            device_id={"row": target(TWIN)}, device_id_type=pl.DeviceIdType.MESH).wait_recv()
+
+    def maybe(way, act):
+        pl.when(exists(way))(act)
+
+    kept = pltpu.make_async_copy(own, spread.at[pl.ds(me * count, count)], own_sem)
+    kept.start()
+
+    @pl.loop(0, parts)
+    def _(s):
+        maybe(UP, lambda: copy(UP, z, y, s, True).start())
+        maybe(DOWN, lambda: copy(DOWN, z, y, s, True).start())
+        copy(ACROSS, z, y, s, True).start()
+        copy(TWIN, z, y, s, True).start()
+
+    def along(d, s, yy, cross):
+        for way, zz, there in ((UP, z - d, z >= d), (DOWN, z + d, z + d < nz)):
+            @pl.when(there)
+            def _(way=way, zz=zz):
+                arrived(zz, yy, s, core)
+                maybe(way, lambda: copy(way, zz, yy, s).start())
+                if cross:
+                    copy(ACROSS, zz, yy, s).start()
+                copy(TWIN, zz, yy, s).start()
+
+    other = ny - 1 - y
+    arrived(z, other, 0, core)
+    maybe(UP, lambda: copy(UP, z, other, 0).start())
+    maybe(DOWN, lambda: copy(DOWN, z, other, 0).start())
+    copy(TWIN, z, other, 0).start()
+
+    def crossed(d, s):
+        if d == 0:
+            arrived(z, other, s, core)
+            copy(TWIN, z, other, s).start()
+        else:
+            for zz, there in ((z - d, z >= d), (z + d, z + d < nz)):
+                @pl.when(there)
+                def _(zz=zz):
+                    arrived(zz, other, s, core)
+                    copy(TWIN, zz, other, s).start()
+
+    for d in range(1, nz):
+        along(d, 0, y, False)
+
+        @pl.loop(1, parts)
+        def _(s):
+            along(d, s, y, True)
+            crossed(d - 1, s)
+
+        along(d, 0, other, False)
+
+    @pl.loop(1, parts)
+    def _(s):
+        crossed(nz - 1, s)
+
+    kept.wait()
+
+    @pl.loop(0, nz * ny * parts)
+    def _(i):
+        arrived(i // (ny * parts), (i // parts) % ny, i % parts, nc - 1 - core)
+
+    def sent(way, zz, yy, s):
+        copy(way, zz, yy, s).wait_send()
+
+    @pl.loop(0, nz * parts)
+    def _(i):
+        zz, s = i // parts, i % parts
+        for yy in range(ny):
+            sent(TWIN, zz, yy, s)
+
+        @pl.when((s > 0) | (zz == z))
+        def _():
+            sent(ACROSS, zz, y, s)
+
+        @pl.when((zz <= z) & (z + 1 < nz))
+        def _():
+            sent(UP, zz, y, s)
+
+        @pl.when((zz >= z) & (z > 0))
+        def _():
+            sent(DOWN, zz, y, s)
+
+        @pl.when((s == 0) & (zz <= z) & (z + 1 < nz))
+        def _():
+            sent(UP, zz, other, s)
+
+        @pl.when((s == 0) & (zz >= z) & (z > 0))
+        def _():
+            sent(DOWN, zz, other, s)
+
+
+def spread_all(own, peers):
+    nc, ny = 2, 2
+    nz, parts = peers // (nc * ny), 8
+    count, width = own.shape[0], own.shape[1]
+    return pl.pallas_call(
+        functools.partial(spread_kernel, nz, ny, nc, parts),
+        out_shape=jax.ShapeDtypeStruct((peers * count, width, width), own.dtype),
+        in_specs=[pl.BlockSpec(memory_space=pl.ANY)],
+        out_specs=pl.BlockSpec(memory_space=pl.ANY),
+        scratch_shapes=[
+            pltpu.SemaphoreType.DMA((4, nz * ny, parts)),
+            pltpu.SemaphoreType.DMA((peers, parts)),
+            pltpu.SemaphoreType.DMA,
+        ],
+        compiler_params=pltpu.CompilerParams(collective_id=0, has_side_effects=True),
+    )(own)
+
+
+def rebuild_kernel(terms, scale, count, requests, first_block, first_request, tl, tf, blk, whole, fresh, square, right0, right1, squares):
+    total = whole.shape[0]
+
+    def term_ids(b):
+        group = b // count
+        lefts = [group * count + tl[b * terms + t] for t in range(terms)]
+        rights = [blk[group * requests + tf[b * terms + t]] for t in range(terms)]
+        return lefts, rights
+
+    def product(left, b):
+        lefts, rights = term_ids(b)
+        lhs = jnp.concatenate([left[i] for i in lefts], axis=1)
+        rhs = jnp.concatenate([whole[i] for i in rights], axis=0)
+        return scale * dot(lhs, rhs)
+
+    @pl.loop(0, total, unroll=8)
+    def _(b):
+        squares[b] = product(whole, b).astype(BF16)
+
+    def purified(b):
+        return (3.0 * squares[b].astype(F32) - 2.0 * product(squares, b)).astype(BF16)
+
+    start = first_block[0]
+
+    @pl.loop(0, count, unroll=8)
+    def _(b):
+        square[b] = squares[start + b]
+        fresh[b] = purified(start + b)
+
+    start_request = first_request[0]
+
+    @pl.loop(0, requests, unroll=8)
+    def _(q):
+        b = blk[start_request + q]
+        right0[q] = whole[b]
+        right1[q] = purified(b)
+
+
 def call(kernel, prefetch, arrays, outs, scratch=(), flops=0):
     whole = pl.BlockSpec(memory_space=pltpu.VMEM)
     smem = pl.BlockSpec(memory_space=pltpu.SMEM)
@@ -170,7 +363,6 @@
     slots = peer_count * slot_count
     tl = term_left.reshape(-1)
     tf = term_fetch.reshape(-1)
-    tr = receive_index[tf]
 
     def shape(n, dtype):
         return jax.ShapeDtypeStruct((n, width, width), dtype)
@@ -186,12 +378,26 @@
         pltpu.VMEM((request_count, width, width), F32),
     ]
     forward = functools.partial(forward_kernel, terms, scale)
-    (out0,) = call(gather_kernel, [send_index], [density_guess], [shape(slots, BF16)])
-    right0 = exchange(out0)
-    first, square1, out1 = call(
-        forward, [tl, tr, send_index], [density_guess, right0],
-        [shape(blocks, BF16), shape(blocks, BF16), shape(slots, BF16)], flops=2 * work)
-    right1 = exchange(out1)
+    if peer_count * blocks * width * width * 2 <= GATHER_BYTES and peer_count % 4 == 0:
+        tables = lax.all_gather(jnp.concatenate([term_left, term_fetch], axis=1), "row", tiled=True)
+        all_left = tables[:, :terms].reshape(-1)
+        all_fetch = tables[:, terms:].reshape(-1)
+        named = req_owner[:, 0] * blocks + req_slot
+        whole = spread_all(density_guess, peer_count)
+        first, square1, right0, right1 = call(
+            functools.partial(rebuild_kernel, terms, scale, blocks, request_count),
+            [(own_index * blocks).reshape(1), (own_index * request_count).reshape(1), all_left, all_fetch, named], [whole],
+            [shape(blocks, BF16), shape(blocks, BF16), shape(request_count, BF16), shape(request_count, BF16)],
+            [pltpu.VMEM((peer_count * blocks, width, width), BF16)], flops=(peer_count + 3) * work)
+        tr = tf
+    else:
+        tr = receive_index[tf]
+        (out0,) = call(gather_kernel, [send_index], [density_guess], [shape(slots, BF16)])
+        right0 = exchange(out0)
+        first, square1, out1 = call(
+            forward, [tl, tr, send_index], [density_guess, right0],
+            [shape(blocks, BF16), shape(blocks, BF16), shape(slots, BF16)], flops=2 * work)
+        right1 = exchange(out1)
     second, square2 = call(
         forward, [tl, tr, send_index], [first, right1],
         [shape(blocks, BF16), shape(blocks, BF16)], flops=2 * work)

time: 259 us -> 239 us (0.923)
  waiting for transfers between devices: 176 us -> 84.9 us
  Pallas kernels: 48.3 us -> 115 us
  blocking collectives: 0 us -> 15.8 us
  starting transfers between devices: 21.3 us -> 9.73 us
    all_to_all x4 -> x2, waiting for transfers between devices: 176 us -> 84.9 us  [exchange(): return lax.all_to_all(x, 'row', split_axis=0, concat_axis=0, tiled=True)]
    pallas_call x0 -> x1, Pallas kernels: none -> 55.2 us  [spread_all(): pl.pallas_call(functools.partial(spread_kernel, nz, ny, nc, parts), out_s...]
    all_gather x0 -> x1, blocking collectives: none -> 15.8 us  [body(): lax.all_gather(jnp.concatenate([term_left, term_fetch], axis=1), 'row', t...]
    all_to_all x4 -> x2, starting transfers between devices: 21.3 us -> 9.73 us  [exchange(): return lax.all_to_all(x, 'row', split_axis=0, concat_axis=0, tiled=True)]
    pallas_call x8 -> x7, Pallas kernels: 48.3 us -> 59.5 us  [call(): pl.pallas_call(kernel, out_shape=outs, in_specs=[smem] * len(prefetch) +...]
    unnamed x18 -> x11, local copies, waits for them, and re-layouts: 5.48 us -> 4.26 us
  transfers between devices with their start and end apart: 4 -> 2, of which waited for: 4 -> 2; matrix products, arithmetic and copies ran while one was open for 2% -> 0% of each run, Pallas kernels for 4% -> 4%
where the time goes in v2:
time: 239 us
  Pallas kernels  115 us (48%)
  waiting for transfers between devices  84.9 us (36%)
  blocking collectives  15.8 us (7%)
  starting transfers between devices  9.73 us (4%)
  local copies, waits for them, and re-layouts  8.88 us (4%)
  other arithmetic  3.89 us (2%)
    all_to_all x2, waiting for transfers between devices, exchange(): return lax.all_to_all(x, 'row', split_axis=0, concat_axis=0, tiled=True)  84.9 us
    pallas_call x7, Pallas kernels, call(): pl.pallas_call(kernel, out_shape=outs, in_specs=[smem] * len(prefetch) +...  59.5 us
    pallas_call x1, Pallas kernels, spread_all(): pl.pallas_call(functools.partial(spread_kernel, nz, ny, nc, parts), out_s...  55.2 us
    all_gather x1, blocking collectives, body(): lax.all_gather(jnp.concatenate([term_left, term_fetch], axis=1), 'row', t...  15.8 us
    all_to_all x2, starting transfers between devices, exchange(): return lax.all_to_all(x, 'row', split_axis=0, concat_axis=0, tiled=True)  9.73 us
  transfers between devices with their start and end apart: 2, of which 2 were waited for; matrix products, arithmetic and copies ran while one was open for 0% of the time, Pallas kernels for 4%

profile of v2, /device:TPU:15, one launch (start us, length us, event | category | flops | bytes accessed | tf_op | source)
XLA Modules:
  0.0 238.7 jit_solution(8675951550014196764)
XLA Ops:
  0.6 0.8 copy.20
  1.4 0.7 add_bitcast_fusion
  2.1 0.8 copy.21
  2.9 0.7 broadcast_multiply_fusion
  3.5 0.7 compare_reduce_fusion
  4.2 15.8 %all-gather = s32[16,16,8]{1,2,0:T(8,128)S(1)} all-gather(s32[1,16,8]{1,2,0:T(8,128)S(1)} %add_bitcast_fusion), channel_id=1, replica_groups=mesh['groups'=2,'row'=16] {'row'}, dimensions={0}, use_global_device_ids=true | all-gather | bytes 8704 | tf_op jit(solution)/shard_map/all_gather | solution.py:382
  20.3 0.7 reshape.59.tl
  21.2 0.7 reshape.60.tf
  21.9 55.2 %shard_map.77.whole = bf16[256,128,128]{2,1,0:T(8,128)(2,1)} custom-call(bf16[16,128,128]{2,1,0:T(8,128)(2,1)} %dens.1), custom_call_target="tpu_custom_call" | custom-call | tf_op jit(solution)/shard_map/pallas_call | solution.py:285
  77.2 0.5 add.14.blk
  77.8 0.2 reduce_window_sum.11
  78.0 0.1 select_reduce_fusion
  78.3 0.7 reshape.56.index
  78.9 0.6 reshape.54.tl
  79.6 0.6 reshape.55.tr.tf
  80.3 0.2 convert_reduce_fusion
  80.4 0.6 multiply_add_fusion.rix
  81.0 21.5 %shard_map.78 = (bf16[16,128,128]{2,1,0:T(8,128)(2,1)}, bf16[16,128,128]{2,1,0:T(8,128)(2,1)}, bf16[32,128,128]{2,1,0:T(8,128)(2,1)}, bf16[32,128,128]{2,1,0:T(8,128)(2,1)}) custom-call(s32[1]{0:T(128)} %bitcast.first_block, s32[1]{0:T(128)} %bitcast.1.first_request, s32[1024]{0:T(1024)} %reshape.59.tl, s32[1024]{0:T(1024)} %reshape.60.tf, s32[512]{0:T(512)} %add.14.blk, ...), custom_call_target="tpu_custom_call" | custom-call | flops 5100273664 | bytes 8388608 | tf_op jit(solution)/shard_map/pallas_call | solution.py:341
  102.5 4.5 %shard_map.79 = (bf16[16,128,128]{2,1,0:T(8,128)(2,1)}, bf16[16,128,128]{2,1,0:T(8,128)(2,1)}) custom-call(s32[64]{0:T(128)} %reshape.54.tl, s32[64]{0:T(128)} %reshape.55.tr.tf, s32[64]{0:T(128)} %reshape.56.index, bf16[16,128,128]{2,1,0:T(8,128)(2,1)} %get-tuple-element.12.dens, bf16[32,128,128]{2,1,0:T(8,128)(2,1)} %get-tuple-element.13.right), custom_call_target="tpu_custom_call" | custom-call | flops 536870912 | bytes 1572864 | tf_op jit(solution)/shard_map/pallas_call | solution.py:341
  107.1 9.1 %shard_map.80 = (bf16[16,128,128]{2,1,0:T(8,128)(2,1)}, bf16[64,128,128]{2,1,0:T(8,128)(2,1)}) custom-call(s32[64]{0:T(128)} %reshape.54.tl, s32[64]{0:T(128)} %reshape.55.tr.tf, s32[64]{0:T(128)} %reshape.55.tr.tf, s32[32]{0:T(128)} %multiply_add_fusion.rix, bf16[16,128,128]{2,1,0:T(8,128)(2,1)} %get-tuple-element.12.dens, ...), custom_call_target="tpu_custom_call" | custom-call | flops 805306368 | bytes 2621440 | tf_op jit(solution)/shard_map/pallas_call | solution.py:341
  116.2 4.8 %all-to-all-start = ((bf16[64,128,128]{2,1,0:T(8,128)(2,1)}), bf16[64,128,128]{2,1,0:T(8,128)(2,1)S(1)}, u32[]{:S(2)}, u32[]{:S(2)}) async-start(bf16[64,128,128]{2,1,0:T(8,128)(2,1)} %get-tuple-element.19), calls=%async_computation | async-start | bytes 4194304 | tf_op jit(solution)/shard_map/all_to_all | solution.py:371
  120.9 0.1 fusion.1
  121.2 0.6 reshape.61.valid
  121.7 4.5 %shard_map.81.local = f32[16,128,128]{2,1,0:T(8,128)} custom-call(s32[64]{0:T(128)} %reshape.54.tl, s32[64]{0:T(128)} %reshape.55.tr.tf, bf16[16,128,128]{2,1,0:T(8,128)(2,1)} %get-tuple-element.18.sqcot, bf16[32,128,128]{2,1,0:T(8,128)(2,1)} %get-tuple-element.13.right), custom_call_target="tpu_custom_call" | custom-call | flops 268435456 | bytes 1572864 | tf_op jit(solution)/shard_map/pallas_call | solution.py:341
  126.3 42.1 %all-to-all-done.returned = bf16[64,128,128]{2,1,0:T(8,128)(2,1)S(1)} async-done(((bf16[64,128,128]{2,1,0:T(8,128)(2,1)}), bf16[64,128,128]{2,1,0:T(8,128)(2,1)S(1)}, u32[]{:S(2)}, u32[]{:S(2)}) %all-to-all-start) | async-done | bytes 2097184 | tf_op jit(solution)/shard_map/all_to_all | solution.py:371
  168.4 1.3 copy-done.1
  169.7 11.2 %shard_map.82 = (bf16[16,128,128]{2,1,0:T(8,128)(2,1)}, bf16[64,128,128]{2,1,0:T(8,128)(2,1)}) custom-call(s32[64]{0:T(128)} %reshape.54.tl, s32[64]{0:T(128)} %reshape.55.tr.tf, s32[64]{0:T(128)} %reshape.55.tr.tf, s32[32]{0:T(128)} %multiply_add_fusion.rix, s32[64]{0:T(128)} %reshape.56.index, s32[64]{0:T(128)} %reshape.61.valid, ...), custom_call_target="tpu_custom_call" | custom-call | flops 805306368 | bytes 5242880 | tf_op jit(solution)/shard_map/pallas_call | solution.py:341
  180.9 5.0 %all-to-all-start.1 = ((bf16[64,128,128]{2,1,0:T(8,128)(2,1)}), bf16[64,128,128]{2,1,0:T(8,128)(2,1)S(1)}, u32[]{:S(2)}, u32[]{:S(2)}) async-start(bf16[64,128,128]{2,1,0:T(8,128)(2,1)} %get-tuple-element.21), calls=%async_computation.1 | async-start | bytes 4194304 | tf_op jit(solution)/shard_map/all_to_all | solution.py:371
  185.8 4.6 %shard_map.83.local = f32[16,128,128]{2,1,0:T(8,128)} custom-call(s32[64]{0:T(128)} %reshape.54.tl, s32[64]{0:T(128)} %reshape.55.tr.tf, bf16[16,128,128]{2,1,0:T(8,128)(2,1)} %get-tuple-element.20.sqcot, bf16[32,128,128]{2,1,0:T(8,128)(2,1)} %get-tuple-element.16.right), custom_call_target="tpu_custom_call" | custom-call | flops 268435456 | bytes 1572864 | tf_op jit(solution)/shard_map/pallas_call | solution.py:341
  190.4 42.9 %all-to-all-done.1.returned = bf16[64,128,128]{2,1,0:T(8,128)(2,1)S(1)} async-done(((bf16[64,128,128]{2,1,0:T(8,128)(2,1)}), bf16[64,128,128]{2,1,0:T(8,128)(2,1)S(1)}, u32[]{:S(2)}, u32[]{:S(2)}) %all-to-all-start.1) | async-done | bytes 2097184 | tf_op jit(solution)/shard_map/all_to_all | solution.py:371
  233.3 1.3 copy-done
  234.6 4.1 %shard_map.84 = f32[16,128,128]{2,1,0:T(8,128)} custom-call(s32[64]{0:T(128)} %reshape.56.index, s32[64]{0:T(128)} %reshape.61.valid, f32[16,128,128]{2,1,0:T(8,128)} %shard_map.83.local, bf16[64,128,128]{2,1,0:T(8,128)(2,1)} %copy-done), custom_call_target="tpu_custom_call" | custom-call | bytes 3145728 | tf_op jit(solution)/shard_map/pallas_call | solution.py:341
  (19 shorter events, 0.8 us)
Async XLA Ops:
  21.9 55.2 %copy-start.3 = (s32[512]{0:T(512)S(1)}, s32[512]{0:T(512)}, u32[]{:S(2)}) copy-start(s32[512]{0:T(512)} %param.11) | copy-start | bytes 6148
  21.9 58.3 %copy-start.2 = (s32[512,1]{0,1:T(1,128)S(1)}, s32[512,1]{0,1:T(1,128)}, u32[]{:S(2)}) copy-start(s32[512,1]{0,1:T(1,128)} %param.10) | copy-start | bytes 6148
  116.2 52.2 %all-to-all-start = ((bf16[64,128,128]{2,1,0:T(8,128)(2,1)}), bf16[64,128,128]{2,1,0:T(8,128)(2,1)S(1)}, u32[]{:S(2)}, u32[]{:S(2)}) async-start(bf16[64,128,128]{2,1,0:T(8,128)(2,1)} %get-tuple-element.19), calls=%async_computation | async-start | bytes 4194304 | tf_op jit(solution)/shard_map/all_to_all | solution.py:371
  168.4 1.3 copy-start.1
  180.9 52.4 %all-to-all-start.1 = ((bf16[64,128,128]{2,1,0:T(8,128)(2,1)}), bf16[64,128,128]{2,1,0:T(8,128)(2,1)S(1)}, u32[]{:S(2)}, u32[]{:S(2)}) async-start(bf16[64,128,128]{2,1,0:T(8,128)(2,1)} %get-tuple-element.21), calls=%async_computation.1 | async-start | bytes 4194304 | tf_op jit(solution)/shard_map/all_to_all | solution.py:371
  233.3 1.4 copy-start

commit v3 on v2

v3 whole, which is shorter than its diff:
```python
import functools

import jax
import jax.numpy as jnp
from jax import lax
from jax.experimental import pallas as pl
from jax.experimental.pallas import tpu as pltpu
from jax.sharding import PartitionSpec as P

F32 = jnp.float32
BF16 = jnp.bfloat16
VMEM_LIMIT = 56 * 1024 * 1024
GATHER_BYTES = 16 * 1024 * 1024


def owner_tables(req_owner, req_slot, own_index, peer_count, slot_count, request_count):
    owners_all = req_owner[:, 0].reshape(peer_count, request_count)
    slots_all = req_slot.reshape(peer_count, request_count)
    mine = owners_all == own_index
    ranks = jnp.cumsum(mine.astype(jnp.int32), axis=1) - 1
    slot_ids = jnp.arange(slot_count, dtype=jnp.int32)
    chosen = mine[:, None, :] & (ranks[:, None, :] == slot_ids[None, :, None])
    send_index = jnp.sum(jnp.where(chosen, slots_all[:, None, :], 0), axis=2).reshape(-1)
    own_owners = lax.dynamic_slice_in_dim(req_owner[:, 0], own_index * request_count, request_count)
    request_ids = jnp.arange(request_count, dtype=jnp.int32)
    earlier = (own_owners[:, None] == own_owners[None, :]) & (
        request_ids[None, :] < request_ids[:, None]
    )
    own_rank = jnp.sum(earlier.astype(jnp.int32), axis=1)
    receive_index = own_owners * slot_count + own_rank
    return (send_index, receive_index)


def dot(a, b):
    return jnp.dot(a, b, preferred_element_type=F32)


def dot_rt(a, b):
    return lax.dot_general(a, b, (((1,), (1,)), ((), ())), preferred_element_type=F32)


def forward_sums(left, right, tl, tr, b, terms):
    lhs = jnp.concatenate([left[tl[b, t]] for t in range(terms)], axis=1)
    rhs = jnp.concatenate([right[tr[b, t]] for t in range(terms)], axis=0)
    return dot(lhs, rhs)


def left_adjoint(cots, right, tl, tr, acc, terms):
    acc[...] = jnp.zeros_like(acc)

    @pl.loop(0, cots.shape[0], unroll=8)
    def _(b):
        rhs = jnp.concatenate([right[tr[b, t]] for t in range(terms)], axis=0)
        piece = dot_rt(cots[b], rhs)
        width = cots.shape[2]
        for t in range(terms):
            acc[tl[b, t]] += piece[:, t * width:(t + 1) * width]


def gather_kernel(index, blocks, out):
    @pl.loop(0, out.shape[0], unroll=4)
    def _(s):
        out[s] = blocks[index[s]]


def square_phase(terms, scale, tl, tr, dens, right, square):
    @pl.loop(0, dens.shape[0], unroll=16)
    def _(b):
        square[b] = (scale * forward_sums(dens, right, tl, tr, b, terms)).astype(BF16)


def fresh_phase(terms, scale, tl, tr, square, right, fresh):
    @pl.loop(0, square.shape[0], unroll=16)
    def _(b):
        cube = scale * forward_sums(square, right, tl, tr, b, terms)
        fresh[b] = (3.0 * square[b].astype(F32) - 2.0 * cube).astype(BF16)


def forward_kernel(terms, scale, tl, tr, index, dens, right, fresh, square, out):
    square_phase(terms, scale, tl, tr, dens, right, square)
    fresh_phase(terms, scale, tl, tr, square, right, fresh)
    gather_kernel(index, fresh, out)


def cot_phase(terms, scale, tl, tr, tf, rix, dens, square, right, cot, sqcot, sendback, acc, cube, both, racc):
    blocks, width = dens.shape[0], dens.shape[2]

    @pl.loop(0, blocks, unroll=4)
    def _(b):
        cube[b] = (-2.0 * cot[b].astype(F32)).astype(BF16)
        both[b] = jnp.concatenate([square[b].T, dens[b].T], axis=1)

    left_adjoint(cube, right, tl, tr, acc, terms)

    @pl.loop(0, blocks, unroll=4)
    def _(b):
        sqcot[b] = (3.0 * cot[b].astype(F32) + scale * acc[b]).astype(BF16)

    racc[...] = jnp.zeros_like(racc)

    @pl.loop(0, blocks, unroll=8)
    def _(b):
        lhs = jnp.concatenate([both[tl[b, t]] for t in range(terms)], axis=0)
        rhs = jnp.concatenate([cube[b], sqcot[b]], axis=0)
        piece = dot(lhs, rhs)
        for t in range(terms):
            racc[tf[b, t]] += piece[t * width:(t + 1) * width]

    @pl.loop(0, sendback.shape[0], unroll=4)
    def _(s):
        sendback[s] = jnp.zeros(sendback.shape[1:], BF16)

    @pl.loop(0, racc.shape[0], unroll=4)
    def _(q):
        sendback[rix[q]] = (scale * racc[q]).astype(BF16)


def reverse_kernel(terms, scale, tl, tr, tf, rix, dens, right, cot, square, sqcot, sendback, acc, cube, both, racc):
    square_phase(terms, scale, tl, tr, dens, right, square)
    cot_phase(terms, scale, tl, tr, tf, rix, dens, square, right, cot, sqcot, sendback, acc, cube, both, racc)


def collect(index, returned, grad):
    @pl.loop(0, returned.shape[0], unroll=8)
    def _(s):
        grad[index[s]] += returned[s].astype(F32)


def chained_kernel(terms, scale, tl, tr, tf, rix, index, dens, square, right, local, returned, sqcot, sendback, acc, cube, both, racc, cot):
    acc[...] = local[...]
    collect(index, returned, acc)
    cot[...] = acc[...].astype(BF16)
    cot_phase(terms, scale, tl, tr, tf, rix, dens, square, right, cot, sqcot, sendback, acc, cube, both, racc)


def local_kernel(terms, scale, tl, tr, sqcot, right, grad):
    left_adjoint(sqcot, right, tl, tr, grad, terms)
    grad[...] = scale * grad[...]


def final_kernel(index, local, returned, grad):
    grad[...] = local[...]
    collect(index, returned, grad)


def spread_kernel(nz, ny, nc, parts, own, own_tab, spread, tabs, send_sem, recv_sem, own_sem):
    me = lax.axis_index("row")
    core, y, z = me % nc, (me // nc) % ny, me // (nc * ny)
    count = own.shape[0]
    size = count // parts
    UP, DOWN, ACROSS, TWIN = 0, 1, 2, 3
    steps = {UP: nc * ny, DOWN: -nc * ny}

    def target(way):
        if way == ACROSS:
            return (z * ny + (ny - 1 - y)) * nc + core
        if way == TWIN:
            return (z * ny + y) * nc + (nc - 1 - core)
        return me + steps[way]

    def exists(way):
        return {UP: z + 1 < nz, DOWN: z > 0}[way]

    barrier = pltpu.get_barrier_semaphore()

    def greet(way):
        pl.semaphore_signal(barrier, inc=1, device_id={"row": target(way)}, device_id_type=pl.DeviceIdType.MESH)

    for way in (UP, DOWN):
        pl.when(exists(way))(functools.partial(greet, way))
    for way in (ACROSS, TWIN):
        greet(way)
    pl.semaphore_wait(barrier, 2 + (z + 1 < nz).astype(jnp.int32) + (z > 0).astype(jnp.int32))

    TAB = parts

    def place_of(origin, s):
        if s is TAB:
            return tabs.at[origin]
        return spread.at[pl.ds(origin * count + s * size, size)]

    def copy(way, zz, yy, s, from_own=False):
        origin = (zz * ny + yy) * nc + core
        place = source = place_of(origin, s)
        if from_own:
            source = own_tab if s is TAB else own.at[pl.ds(s * size, size)]
        return pltpu.make_async_remote_copy(
            src_ref=source, dst_ref=place,
            send_sem=send_sem.at[way, zz * ny + yy, s], recv_sem=recv_sem.at[origin, s],
            device_id={"row": target(way)}, device_id_type=pl.DeviceIdType.MESH)

    def arrived(zz, yy, s, plane):
        origin = (zz * ny + yy) * nc + plane
        place = place_of(origin, s)
        pltpu.make_async_remote_copy(
            src_ref=place, dst_ref=place,
            send_sem=send_sem.at[TWIN, 0, 0], recv_sem=recv_sem.at[origin, s],
            device_id={"row": target(TWIN)}, device_id_type=pl.DeviceIdType.MESH).wait_recv()

    def maybe(way, act):
        pl.when(exists(way))(act)

    kept = pltpu.make_async_copy(own, spread.at[pl.ds(me * count, count)], own_sem.at[0])
    kept.start()
    kept_tab = pltpu.make_async_copy(own_tab, tabs.at[me], own_sem.at[1])
    kept_tab.start()

    def begin(s):
        maybe(UP, lambda: copy(UP, z, y, s, True).start())
        maybe(DOWN, lambda: copy(DOWN, z, y, s, True).start())
        copy(ACROSS, z, y, s, True).start()
        copy(TWIN, z, y, s, True).start()

    begin(TAB)
    pl.loop(0, parts)(begin)

    def along(d, s, yy, cross):
        for way, zz, there in ((UP, z - d, z >= d), (DOWN, z + d, z + d < nz)):
            @pl.when(there)
            def _(way=way, zz=zz):
                arrived(zz, yy, s, core)
                maybe(way, lambda: copy(way, zz, yy, s).start())
                if cross:
                    copy(ACROSS, zz, yy, s).start()
                copy(TWIN, zz, yy, s).start()

    other = ny - 1 - y
    arrived(z, other, 0, core)
    maybe(UP, lambda: copy(UP, z, other, 0).start())
    maybe(DOWN, lambda: copy(DOWN, z, other, 0).start())
    copy(TWIN, z, other, 0).start()

    def crossed(d, s):
        if d == 0:
            arrived(z, other, s, core)
            copy(TWIN, z, other, s).start()
        else:
            for zz, there in ((z - d, z >= d), (z + d, z + d < nz)):
                @pl.when(there)
                def _(zz=zz):
                    arrived(zz, other, s, core)
                    copy(TWIN, zz, other, s).start()

    for d in range(1, nz):
        along(d, 0, y, False)
        along(d, TAB, y, True)
        crossed(d - 1, TAB)

        @pl.loop(1, parts)
        def _(s):
            along(d, s, y, True)
            crossed(d - 1, s)

        along(d, 0, other, False)

    crossed(nz - 1, TAB)

    @pl.loop(1, parts)
    def _(s):
        crossed(nz - 1, s)

    kept.wait()
    kept_tab.wait()

    @pl.loop(0, nz * ny)
    def _(i):
        arrived(i // ny, i % ny, TAB, nc - 1 - core)

        @pl.loop(0, parts)
        def _(s):
            arrived(i // ny, i % ny, s, nc - 1 - core)

    def sent(way, zz, yy, s):
        copy(way, zz, yy, s).wait_send()

    def finish(zz, s, first):
        for yy in range(ny):
            sent(TWIN, zz, yy, s)

        @pl.when(jnp.logical_or(jnp.logical_not(first), zz == z))
        def _():
            sent(ACROSS, zz, y, s)

        @pl.when((zz <= z) & (z + 1 < nz))
        def _():
            sent(UP, zz, y, s)

        @pl.when((zz >= z) & (z > 0))
        def _():
            sent(DOWN, zz, y, s)

        if s is not TAB:
            @pl.when(first & (zz <= z) & (z + 1 < nz))
            def _():
                sent(UP, zz, other, s)

            @pl.when(first & (zz >= z) & (z > 0))
            def _():
                sent(DOWN, zz, other, s)

    @pl.loop(0, nz)
    def _(zz):
        finish(zz, TAB, False)

        @pl.loop(0, parts)
        def _(s):
            finish(zz, s, s == 0)


def spread_all(own, own_tab, peers):
    nc, ny = 2, 2
    nz, parts = peers // (nc * ny), 8
    count, width = own.shape[0], own.shape[1]
    return pl.pallas_call(
        functools.partial(spread_kernel, nz, ny, nc, parts),
        out_shape=[
            jax.ShapeDtypeStruct((peers * count, width, width), own.dtype),
            jax.ShapeDtypeStruct((peers,) + own_tab.shape, own_tab.dtype),
        ],
        in_specs=[pl.BlockSpec(memory_space=pl.ANY)] * 2,
        out_specs=[pl.BlockSpec(memory_space=pl.ANY)] * 2,
        scratch_shapes=[
            pltpu.SemaphoreType.DMA((4, nz * ny, parts + 1)),
            pltpu.SemaphoreType.DMA((peers, parts + 1)),
            pltpu.SemaphoreType.DMA((2,)),
        ],
        compiler_params=pltpu.CompilerParams(collective_id=0, has_side_effects=True),
    )(own, own_tab)


def rebuild_kernel(terms, scale, row, tl, tf, rix, tabs, blk, whole, cot, fresh, square, right0, right1, square2, sqcot, sendback, acc, cube, both, racc, parts):
    count, requests = fresh.shape[0], right0.shape[0]
    me = row[0]

    def term_ids(b):
        group, at = b // count, (b % count) * 2 * terms
        lefts = [group * count + tabs[group, 0, at + t] for t in range(terms)]
        rights = [blk[group * requests + tabs[group, 0, at + terms + t]] for t in range(terms)]
        return lefts, rights

    def product(left, lefts, rights):
        lhs = jnp.concatenate([left[i] for i in lefts], axis=1)
        rhs = jnp.concatenate([whole[i] for i in rights], axis=0)
        return scale * dot(lhs, rhs)

    @pl.loop(0, requests, unroll=2)
    def _(q):
        b = blk[me * requests + q]
        right0[q] = whole[b]
        lefts, _ = term_ids(b)
        for t, i in enumerate(lefts + [b]):
            parts[q * (terms + 1) + t] = product(whole, *term_ids(i)).astype(BF16)

    @pl.loop(0, requests, unroll=8)
    def _(q):
        _, rights = term_ids(blk[me * requests + q])
        at = q * (terms + 1)
        cubed = product(parts, [at + t for t in range(terms)], rights)
        right1[q] = (3.0 * parts[at + terms].astype(F32) - 2.0 * cubed).astype(BF16)

    square_phase(terms, scale, tl, tf, whole.at[pl.ds(me * count, count)], right0, square)
    fresh_phase(terms, scale, tl, tf, square, right0, fresh)
    reverse_kernel(terms, scale, tl, tf, tf, rix, fresh, right1, cot, square2, sqcot, sendback, acc, cube, both, racc)


def call(kernel, prefetch, arrays, outs, scratch=(), flops=0):
    whole = pl.BlockSpec(memory_space=pltpu.VMEM)
    smem = pl.BlockSpec(memory_space=pltpu.SMEM)
    moved = sum(a.size * a.dtype.itemsize for a in arrays)
    return pl.pallas_call(
        kernel,
        out_shape=outs,
        in_specs=[smem] * len(prefetch) + [whole] * len(arrays),
        out_specs=[whole] * len(outs),
        scratch_shapes=list(scratch),
        cost_estimate=pl.CostEstimate(flops=flops, bytes_accessed=moved, transcendentals=0),
        compiler_params=pltpu.CompilerParams(vmem_limit_bytes=VMEM_LIMIT),
    )(*prefetch, *arrays)


def body(density_guess, cotangent, term_left, term_fetch, req_owner, req_slot):
    peer_count = lax.axis_size("row")
    own_index = lax.axis_index("row")
    request_count = req_owner.shape[0] // peer_count
    slot_count = max(2, 2 * request_count // peer_count)
    blocks, width = density_guess.shape[0], density_guess.shape[1]
    terms = term_left.shape[1]
    scale = float(width * terms) ** (-0.5)
    send_index, receive_index = owner_tables(
        req_owner, req_slot, own_index, peer_count, slot_count, request_count
    )
    slots = peer_count * slot_count
    tl, tf = term_left, term_fetch

    def shape(n, dtype):
        return jax.ShapeDtypeStruct((n, width, width), dtype)

    def exchange(x):
        return lax.all_to_all(x, "row", split_axis=0, concat_axis=0, tiled=True)

    work = 2 * blocks * terms * width ** 3
    common = [
        pltpu.VMEM((blocks, width, width), F32),
        pltpu.VMEM((blocks, width, width), BF16),
        pltpu.VMEM((blocks, width, 2 * width), BF16),
        pltpu.VMEM((request_count, width, width), F32),
    ]
    if peer_count * blocks * width * width * 2 <= GATHER_BYTES and peer_count % 4 == 0:
        tr = tf
        own_tab = jnp.concatenate([term_left, term_fetch], axis=1).reshape(1, -1)
        own_tab = jnp.broadcast_to(own_tab, (8, own_tab.shape[1]))
        named = req_owner[:, 0] * blocks + req_slot
        whole, tabs = spread_all(density_guess, own_tab, peer_count)
        first, square1, right0, right1, square2, sqcot2, back2 = call(
            functools.partial(rebuild_kernel, terms, scale),
            [own_index.reshape(1), tl, tf, receive_index, tabs, named], [whole, cotangent],
            [shape(blocks, BF16), shape(blocks, BF16), shape(request_count, BF16), shape(request_count, BF16),
             shape(blocks, BF16), shape(blocks, BF16), shape(slots, BF16)],
            common + [pltpu.VMEM((request_count * (terms + 1), width, width), BF16)], flops=(peer_count + 6) * work)
    else:
        tr = receive_index[tf]
        (out0,) = call(gather_kernel, [send_index], [density_guess], [shape(slots, BF16)])
        right0 = exchange(out0)
        first, square1, out1 = call(
            functools.partial(forward_kernel, terms, scale), [tl, tr, send_index], [density_guess, right0],
            [shape(blocks, BF16), shape(blocks, BF16), shape(slots, BF16)], flops=2 * work)
        right1 = exchange(out1)
        square2, sqcot2, back2 = call(
            functools.partial(reverse_kernel, terms, scale), [tl, tr, tf, receive_index],
            [first, right1, cotangent],
            [shape(blocks, BF16), shape(blocks, BF16), shape(slots, BF16)], common, flops=4 * work)
    returned2 = exchange(back2)
    (second,) = call(
        functools.partial(fresh_phase, terms, scale), [tl, tr], [square2, right1], [shape(blocks, BF16)], flops=work)
    local = functools.partial(local_kernel, terms, scale)
    (local2,) = call(local, [tl, tr], [sqcot2, right1], [shape(blocks, F32)], flops=work)
    sqcot1, back1 = call(
        functools.partial(chained_kernel, terms, scale),
        [tl, tr, tf, receive_index, send_index],
        [density_guess, square1, right0, local2, returned2],
        [shape(blocks, BF16), shape(slots, BF16)],
        common + [pltpu.VMEM((blocks, width, width), BF16)], flops=3 * work)
    returned1 = exchange(back1)
    (local1,) = call(local, [tl, tr], [sqcot1, right0], [shape(blocks, F32)], flops=work)
    (grad,) = call(final_kernel, [send_index], [local1, returned1], [shape(blocks, F32)])
    return (second, grad)


def solution(mesh):
    placed = (
        P(("groups", "row"), None, None),
        P(("groups", "row"), None, None),
        P(("groups", "row"), None),
        P(("groups", "row"), None),
        P("groups", None),
        P("groups"),
    )
    return jax.shard_map(
        body,
        mesh=mesh,
        in_specs=placed,
        out_specs=(P(("groups", "row"), None, None), P(("groups", "row"), None, None)),
        check_vma=False,
    )
```

time: 239 us -> 204 us (0.85)
  Pallas kernels: 115 us -> 95.5 us
  blocking collectives: 15.8 us -> 0 us
    all_gather x1 -> x0, blocking collectives: 15.8 us -> none  [body(): lax.all_gather(jnp.concatenate([term_left, term_fetch], axis=1), 'row', t...]
    pallas_call x7 -> x6, Pallas kernels: 59.5 us -> 45.1 us  [call(): pl.pallas_call(kernel, out_shape=outs, in_specs=[smem] * len(prefetch) +...]
    pallas_call x1, Pallas kernels: 55.2 us -> 50.4 us  [spread_all(): pl.pallas_call(functools.partial(spread_kernel, nz, ny, nc, parts), out_s...]
    reshape x4 -> x0, local copies, waits for them, and re-layouts: 2.68 us -> none  [the longest x1 0.72 us: body(): all_left = tables[:, :terms].reshape(-1)]
    unnamed x11 -> x10, local copies, waits for them, and re-layouts: 4.26 us -> 5.36 us
  transfers between devices with their start and end apart: 2 -> 2, of which waited for: 2 -> 2; matrix products, arithmetic and copies ran while one was open for 0% -> 1% of each run, Pallas kernels for 4% -> 5%
where the time goes in v3:
time: 204 us; the launch traced here: 203 us
  Pallas kernels  95.5 us (47%)
  waiting for transfers between devices  83.7 us (41%)
  starting transfers between devices  11.3 us (6%)
  local copies, waits for them, and re-layouts  7.76 us (4%)
  other arithmetic  4.53 us (2%)
    all_to_all x2, waiting for transfers between devices, exchange(): return lax.all_to_all(x, 'row', split_axis=0, concat_axis=0, tiled=True)  83.7 us
    pallas_call x1, Pallas kernels, spread_all(): pl.pallas_call(functools.partial(spread_kernel, nz, ny, nc, parts), out_s...  50.4 us
    pallas_call x6, Pallas kernels, call(): pl.pallas_call(kernel, out_shape=outs, in_specs=[smem] * len(prefetch) +...  45.1 us
    all_to_all x2, starting transfers between devices, exchange(): return lax.all_to_all(x, 'row', split_axis=0, concat_axis=0, tiled=True)  11.3 us
    unnamed x10, local copies, waits for them, and re-layouts  5.36 us
  transfers between devices with their start and end apart: 2, of which 2 were waited for; matrix products, arithmetic and copies ran while one was open for 1% of the time, Pallas kernels for 5%

profile of v3, /device:TPU:15, one launch (start us, length us, event | category | flops | bytes accessed | tf_op | source)
XLA Modules:
  0.0 203.4 jit_solution(11669001487993816083)
XLA Ops:
  0.6 1.4 copy.35.tl
  2.0 1.4 copy.36.tf.tr
  3.3 0.7 pad_add_fusion
  4.0 0.7 broadcast_multiply_fusion
  4.7 0.7 dynamic-slice_bitcast_fusion
  5.5 0.2 convert_reduce_fusion
  5.6 1.3 multiply_add_fusion.rix
  7.0 0.1 copy.32
  7.0 0.1 broadcast_in_dim.28
  7.1 0.6 broadcast_in_dim.29.own_tab
  7.7 50.4 %shard_map.77 = (bf16[256,128,128]{2,1,0:T(8,128)(2,1)}, s32[16,8,128]{2,1,0:T(8,128)}) custom-call(bf16[16,128,128]{2,1,0:T(8,128)(2,1)} %dens.1, s32[8,128]{1,0:T(8,128)} %broadcast_in_dim.29.own_tab), custom_call_target="tpu_custom_call" | custom-call | tf_op jit(solution)/shard_map/pallas_call | solution.py:314
  58.1 1.3 add.16.blk
  59.4 23.2 %shard_map.78 = (bf16[16,128,128]{2,1,0:T(8,128)(2,1)}, bf16[16,128,128]{2,1,0:T(8,128)(2,1)}, bf16[32,128,128]{2,1,0:T(8,128)(2,1)}, bf16[32,128,128]{2,1,0:T(8...) custom-call(s32[1]{0:T(128)} %bitcast.row, ...), custom_call_target="tpu_custom_call" | custom-call | flops 5905580032 | bytes 8912896 | tf_op jit(solution)/shard_map/pallas_call | solution.py:370
  82.6 6.5 %all-to-all-start = ((bf16[64,128,128]{2,1,0:T(8,128)(2,1)}), bf16[64,128,128]{2,1,0:T(8,128)(2,1)S(1)}, u32[]{:S(2)}, u32[]{:S(2)}) async-start(bf16[64,128,128]{2,1,0:T(8,128)(2,1)} %get-tuple-element.19), calls=%async_computation | async-start | bytes 4194304 | tf_op jit(solution)/shard_map/all_to_all | solution.py:399
  89.1 0.0 copy-done.3
  89.1 0.1 broadcast_in_dim.30
  89.2 0.0 copy-done.2
  89.2 0.1 eq.48
  89.3 0.2 reduce_window_sum.11
  89.5 0.2 select_reduce_fusion
  89.7 0.1 copy.37
  89.7 0.7 reshape.39.index
  90.4 3.5 %shard_map.80.local = f32[16,128,128]{2,1,0:T(8,128)} custom-call(s32[16,4]{1,0:T(8,128)} %copy.35.tl, s32[16,4]{1,0:T(8,128)} %copy.36.tf.tr, bf16[16,128,128]{2,1,0:T(8,128)(2,1)} %get-tuple-element.18.sqcot, bf16[32,128,128]{2,1,0:T(8,128)(2,1)} %get-tuple-element.15.right), custom_call_target="tpu_custom_call" | custom-call | flops 268435456 | bytes 1572864 | tf_op jit(solution)/shard_map/pallas_call | solution.py:370
  93.9 42.6 %all-to-all-done.returned = bf16[64,128,128]{2,1,0:T(8,128)(2,1)S(1)} async-done(((bf16[64,128,128]{2,1,0:T(8,128)(2,1)}), bf16[64,128,128]{2,1,0:T(8,128)(2,1)S(1)}, u32[]{:S(2)}, u32[]{:S(2)}) %all-to-all-start) | async-done | bytes 2097184 | tf_op jit(solution)/shard_map/all_to_all | solution.py:399
  136.5 1.3 copy-done
  137.8 8.5 %shard_map.81 = (bf16[16,128,128]{2,1,0:T(8,128)(2,1)}, bf16[64,128,128]{2,1,0:T(8,128)(2,1)}) custom-call(s32[16,4]{1,0:T(8,128)} %copy.35.tl, s32[16,4]{1,0:T(8,128)} %copy.36.tf.tr, s32[16,4]{1,0:T(8,128)} %copy.36.tf.tr, s32[32]{0:T(128)} %multiply_add_fusion.rix, s32[64]{0:T(128)} %reshape.39.index, bf16[16,128,128]{2,1,0:T(8,128)(2,1)} %dens.1, ...), custom_call_target="tpu_custom_call" | custom-call | flops 805306368 | bytes 5242880 | tf_op jit(solution)/shard_map/pallas_call | solution.py:370
  146.3 4.9 %all-to-all-start.1 = ((bf16[64,128,128]{2,1,0:T(8,128)(2,1)}), bf16[64,128,128]{2,1,0:T(8,128)(2,1)S(1)}, u32[]{:S(2)}, u32[]{:S(2)}) async-start(bf16[64,128,128]{2,1,0:T(8,128)(2,1)} %get-tuple-element.21), calls=%async_computation.1 | async-start | bytes 4194304 | tf_op jit(solution)/shard_map/all_to_all | solution.py:399
  151.2 2.9 %shard_map.79 = bf16[16,128,128]{2,1,0:T(8,128)(2,1)} custom-call(s32[16,4]{1,0:T(8,128)} %copy.35.tl, s32[16,4]{1,0:T(8,128)} %copy.36.tf.tr, bf16[16,128,128]{2,1,0:T(8,128)(2,1)} %get-tuple-element.14.square, bf16[32,128,128]{2,1,0:T(8,128)(2,1)} %get-tuple-element.15.right), custom_call_target="tpu_custom_call" | custom-call | flops 268435456 | bytes 1572864 | tf_op jit(solution)/shard_map/pallas_call | solution.py:370
  154.1 3.5 %shard_map.82.local = f32[16,128,128]{2,1,0:T(8,128)} custom-call(s32[16,4]{1,0:T(8,128)} %copy.35.tl, s32[16,4]{1,0:T(8,128)} %copy.36.tf.tr, bf16[16,128,128]{2,1,0:T(8,128)(2,1)} %get-tuple-element.20.sqcot, bf16[32,128,128]{2,1,0:T(8,128)(2,1)} %get-tuple-element.17.right), custom_call_target="tpu_custom_call" | custom-call | flops 268435456 | bytes 1572864 | tf_op jit(solution)/shard_map/pallas_call | solution.py:370
  157.6 41.0 %all-to-all-done.1.returned = bf16[64,128,128]{2,1,0:T(8,128)(2,1)S(1)} async-done(((bf16[64,128,128]{2,1,0:T(8,128)(2,1)}), bf16[64,128,128]{2,1,0:T(8,128)(2,1)S(1)}, u32[]{:S(2)}, u32[]{:S(2)}) %all-to-all-start.1) | async-done | bytes 2097184 | tf_op jit(solution)/shard_map/all_to_all | solution.py:399
  198.6 1.3 copy-done.1
  199.9 3.5 %shard_map.83 = f32[16,128,128]{2,1,0:T(8,128)} custom-call(s32[64]{0:T(128)} %reshape.39.index, f32[16,128,128]{2,1,0:T(8,128)} %shard_map.82.local, bf16[64,128,128]{2,1,0:T(8,128)(2,1)} %copy-done.1), custom_call_target="tpu_custom_call" | custom-call | bytes 3145728 | tf_op jit(solution)/shard_map/pallas_call | solution.py:370
  (7 shorter events, 0.0 us)
Async XLA Ops:
  82.6 6.5 %copy-start.3 = (s32[512]{0:T(512)S(1)}, s32[512]{0:T(512)}, u32[]{:S(2)}) copy-start(s32[512]{0:T(512)} %param.11) | copy-start | bytes 6148
  82.6 6.6 %copy-start.2 = (s32[512,1]{0,1:T(1,128)S(1)}, s32[512,1]{0,1:T(1,128)}, u32[]{:S(2)}) copy-start(s32[512,1]{0,1:T(1,128)} %param.10) | copy-start | bytes 6148
  82.6 53.9 %all-to-all-start = ((bf16[64,128,128]{2,1,0:T(8,128)(2,1)}), bf16[64,128,128]{2,1,0:T(8,128)(2,1)S(1)}, u32[]{:S(2)}, u32[]{:S(2)}) async-start(bf16[64,128,128]{2,1,0:T(8,128)(2,1)} %get-tuple-element.19), calls=%async_computation | async-start | bytes 4194304 | tf_op jit(solution)/shard_map/all_to_all | solution.py:399
  136.5 1.3 copy-start
  146.3 52.3 %all-to-all-start.1 = ((bf16[64,128,128]{2,1,0:T(8,128)(2,1)}), bf16[64,128,128]{2,1,0:T(8,128)(2,1)S(1)}, u32[]{:S(2)}, u32[]{:S(2)}) async-start(bf16[64,128,128]{2,1,0:T(8,128)(2,1)} %get-tuple-element.21), calls=%async_computation.1 | async-start | bytes 4194304 | tf_op jit(solution)/shard_map/all_to_all | solution.py:399
  198.6 1.4 copy-start.1

commit v4 on v3

--- a/solution.py
+++ b/solution.py
@@ -31,6 +31,22 @@
     return (send_index, receive_index)
 
 
+class Rows:
+    def __init__(self, tab, stride, first):
+        self.tab, self.stride, self.first = tab, stride, first
+
+    def __getitem__(self, at):
+        return self.tab[0, at[0] * self.stride + self.first + at[1]]
+
+
+def with_terms(kernel, terms, groups, scale):
+    def run(tab, *rest):
+        tl, tf, tr = (Rows(tab, groups * terms, i * terms) for i in (0, 1, groups - 1))
+        kernel(terms, scale, tl, tr, tf, *rest)
+
+    return run
+
+
 def dot(a, b):
     return jnp.dot(a, b, preferred_element_type=F32)
 
@@ -63,26 +79,26 @@
         out[s] = blocks[index[s]]
 
 
-def square_phase(terms, scale, tl, tr, dens, right, square):
+def square_phase(terms, scale, tl, tr, tf, dens, right, square):
     @pl.loop(0, dens.shape[0], unroll=16)
     def _(b):
         square[b] = (scale * forward_sums(dens, right, tl, tr, b, terms)).astype(BF16)
 
 
-def fresh_phase(terms, scale, tl, tr, square, right, fresh):
+def fresh_phase(terms, scale, tl, tr, tf, square, right, fresh):
     @pl.loop(0, square.shape[0], unroll=16)
     def _(b):
         cube = scale * forward_sums(square, right, tl, tr, b, terms)
         fresh[b] = (3.0 * square[b].astype(F32) - 2.0 * cube).astype(BF16)
 
 
-def forward_kernel(terms, scale, tl, tr, index, dens, right, fresh, square, out):
-    square_phase(terms, scale, tl, tr, dens, right, square)
-    fresh_phase(terms, scale, tl, tr, square, right, fresh)
+def forward_kernel(terms, scale, tl, tr, tf, index, dens, right, fresh, square, out):
+    square_phase(terms, scale, tl, tr, tf, dens, right, square)
+    fresh_phase(terms, scale, tl, tr, tf, square, right, fresh)
     gather_kernel(index, fresh, out)
 
 
-def cot_phase(terms, scale, tl, tr, tf, rix, dens, square, right, cot, sqcot, sendback, acc, cube, both, racc):
+def cot_phase(terms, scale, tl, tr, tf, row, blk, dens, square, right, cot, sqcot, sendback, acc, cube, both, racc, counts):
     blocks, width = dens.shape[0], dens.shape[2]
 
     @pl.loop(0, blocks, unroll=4)
@@ -110,14 +126,24 @@
     def _(s):
         sendback[s] = jnp.zeros(sendback.shape[1:], BF16)
 
-    @pl.loop(0, racc.shape[0], unroll=4)
+    peers, requests = counts.shape[0], racc.shape[0]
+
+    @pl.loop(0, peers)
+    def _(p):
+        counts[p] = 0
+
+    @pl.loop(0, requests, unroll=4)
     def _(q):
-        sendback[rix[q]] = (scale * racc[q]).astype(BF16)
-
-
-def reverse_kernel(terms, scale, tl, tr, tf, rix, dens, right, cot, square, sqcot, sendback, acc, cube, both, racc):
-    square_phase(terms, scale, tl, tr, dens, right, square)
-    cot_phase(terms, scale, tl, tr, tf, rix, dens, square, right, cot, sqcot, sendback, acc, cube, both, racc)
+        owner = blk[row[0] * requests + q] // blocks
+        rank = counts[owner]
+        counts[owner] = rank + 1
+        slot = owner * (sendback.shape[0] // peers) + rank
+        sendback[slot] = (scale * racc[q]).astype(BF16)
+
+
+def reverse_kernel(terms, scale, tl, tr, tf, row, blk, dens, right, cot, square, sqcot, sendback, acc, cube, both, racc, counts):
+    square_phase(terms, scale, tl, tr, tf, dens, right, square)
+    cot_phase(terms, scale, tl, tr, tf, row, blk, dens, square, right, cot, sqcot, sendback, acc, cube, both, racc, counts)
 
 
 def collect(index, returned, grad):
@@ -126,14 +152,14 @@
         grad[index[s]] += returned[s].astype(F32)
 
 
-def chained_kernel(terms, scale, tl, tr, tf, rix, index, dens, square, right, local, returned, sqcot, sendback, acc, cube, both, racc, cot):
+def chained_kernel(terms, scale, tl, tr, tf, row, blk, index, dens, square, right, local, returned, sqcot, sendback, acc, cube, both, racc, counts, cot):
     acc[...] = local[...]
     collect(index, returned, acc)
     cot[...] = acc[...].astype(BF16)
-    cot_phase(terms, scale, tl, tr, tf, rix, dens, square, right, cot, sqcot, sendback, acc, cube, both, racc)
-
-
-def local_kernel(terms, scale, tl, tr, sqcot, right, grad):
+    cot_phase(terms, scale, tl, tr, tf, row, blk, dens, square, right, cot, sqcot, sendback, acc, cube, both, racc, counts)
+
+
+def local_kernel(terms, scale, tl, tr, tf, sqcot, right, grad):
     left_adjoint(sqcot, right, tl, tr, grad, terms)
     grad[...] = scale * grad[...]
 
@@ -241,23 +267,24 @@
                     arrived(zz, other, s, core)
                     copy(TWIN, zz, other, s).start()
 
+    def drain(d):
+        crossed(d, TAB)
+        pl.loop(1, parts)(functools.partial(crossed, d))
+
     for d in range(1, nz):
         along(d, 0, y, False)
         along(d, TAB, y, True)
-        crossed(d - 1, TAB)
 
         @pl.loop(1, parts)
         def _(s):
             along(d, s, y, True)
-            crossed(d - 1, s)
 
         along(d, 0, other, False)
-
-    crossed(nz - 1, TAB)
-
-    @pl.loop(1, parts)
-    def _(s):
-        crossed(nz - 1, s)
+        if d == 1:
+            drain(0)
+
+    for d in range(1, nz):
+        drain(d)
 
     kept.wait()
     kept_tab.wait()
@@ -328,7 +355,7 @@
     )(own, own_tab)
 
 
-def rebuild_kernel(terms, scale, row, tl, tf, rix, tabs, blk, whole, cot, fresh, square, right0, right1, square2, sqcot, sendback, acc, cube, both, racc, parts):
+def rebuild_kernel(terms, scale, tl, tr, tf, row, blk, tabs, whole, cot, fresh, square, right0, right1, square2, sqcot, sendback, acc, cube, both, racc, counts, parts):
     count, requests = fresh.shape[0], right0.shape[0]
     me = row[0]
 
@@ -358,9 +385,9 @@
         cubed = product(parts, [at + t for t in range(terms)], rights)
         right1[q] = (3.0 * parts[at + terms].astype(F32) - 2.0 * cubed).astype(BF16)
 
-    square_phase(terms, scale, tl, tf, whole.at[pl.ds(me * count, count)], right0, square)
-    fresh_phase(terms, scale, tl, tf, square, right0, fresh)
-    reverse_kernel(terms, scale, tl, tf, tf, rix, fresh, right1, cot, square2, sqcot, sendback, acc, cube, both, racc)
+    square_phase(terms, scale, tl, tr, tf, whole.at[pl.ds(me * count, count)], right0, square)
+    fresh_phase(terms, scale, tl, tr, tf, square, right0, fresh)
+    reverse_kernel(terms, scale, tl, tr, tf, row, blk, fresh, right1, cot, square2, sqcot, sendback, acc, cube, both, racc, counts)
 
 
 def call(kernel, prefetch, arrays, outs, scratch=(), flops=0):
@@ -386,11 +413,9 @@
     blocks, width = density_guess.shape[0], density_guess.shape[1]
     terms = term_left.shape[1]
     scale = float(width * terms) ** (-0.5)
-    send_index, receive_index = owner_tables(
-        req_owner, req_slot, own_index, peer_count, slot_count, request_count
-    )
     slots = peer_count * slot_count
-    tl, tf = term_left, term_fetch
+    row = own_index.reshape(1)
+    named = req_owner[:, 0] * blocks + req_slot
 
     def shape(n, dtype):
         return jax.ShapeDtypeStruct((n, width, width), dtype)
@@ -404,44 +429,52 @@
         pltpu.VMEM((blocks, width, width), BF16),
         pltpu.VMEM((blocks, width, 2 * width), BF16),
         pltpu.VMEM((request_count, width, width), F32),
+        pltpu.SMEM((peer_count,), jnp.int32),
     ]
+
+    def packed(*columns):
+        tab = jnp.concatenate(columns, axis=1).reshape(1, -1)
+        return jnp.broadcast_to(tab, (8, tab.shape[1]))
+
+    def routes(owner, slot):
+        return owner_tables(owner, slot, own_index, peer_count, slot_count, request_count)
+
     if peer_count * blocks * width * width * 2 <= GATHER_BYTES and peer_count % 4 == 0:
-        tr = tf
-        own_tab = jnp.concatenate([term_left, term_fetch], axis=1).reshape(1, -1)
-        own_tab = jnp.broadcast_to(own_tab, (8, own_tab.shape[1]))
-        named = req_owner[:, 0] * blocks + req_slot
-        whole, tabs = spread_all(density_guess, own_tab, peer_count)
+        tab, groups = packed(term_left, term_fetch), 2
+        whole, tabs = spread_all(density_guess, tab, peer_count)
         first, square1, right0, right1, square2, sqcot2, back2 = call(
-            functools.partial(rebuild_kernel, terms, scale),
-            [own_index.reshape(1), tl, tf, receive_index, tabs, named], [whole, cotangent],
+            with_terms(rebuild_kernel, terms, groups, scale),
+            [tab, row, named, tabs], [whole, cotangent],
             [shape(blocks, BF16), shape(blocks, BF16), shape(request_count, BF16), shape(request_count, BF16),
              shape(blocks, BF16), shape(blocks, BF16), shape(slots, BF16)],
             common + [pltpu.VMEM((request_count * (terms + 1), width, width), BF16)], flops=(peer_count + 6) * work)
+        owner, slot, back2 = lax.optimization_barrier((req_owner, req_slot, back2))
+        send_index, _ = routes(owner, slot)
     else:
-        tr = receive_index[tf]
+        send_index, receive_index = routes(req_owner, req_slot)
+        tab, groups = packed(term_left, term_fetch, receive_index[term_fetch]), 3
         (out0,) = call(gather_kernel, [send_index], [density_guess], [shape(slots, BF16)])
         right0 = exchange(out0)
         first, square1, out1 = call(
-            functools.partial(forward_kernel, terms, scale), [tl, tr, send_index], [density_guess, right0],
+            with_terms(forward_kernel, terms, groups, scale), [tab, send_index], [density_guess, right0],
             [shape(blocks, BF16), shape(blocks, BF16), shape(slots, BF16)], flops=2 * work)
         right1 = exchange(out1)
         square2, sqcot2, back2 = call(
-            functools.partial(reverse_kernel, terms, scale), [tl, tr, tf, receive_index],
+            with_terms(reverse_kernel, terms, groups, scale), [tab, row, named],
             [first, right1, cotangent],
             [shape(blocks, BF16), shape(blocks, BF16), shape(slots, BF16)], common, flops=4 * work)
     returned2 = exchange(back2)
     (second,) = call(
-        functools.partial(fresh_phase, terms, scale), [tl, tr], [square2, right1], [shape(blocks, BF16)], flops=work)
-    local = functools.partial(local_kernel, terms, scale)
-    (local2,) = call(local, [tl, tr], [sqcot2, right1], [shape(blocks, F32)], flops=work)
+        with_terms(fresh_phase, terms, groups, scale), [tab], [square2, right1], [shape(blocks, BF16)], flops=work)
+    local = with_terms(local_kernel, terms, groups, scale)
+    (local2,) = call(local, [tab], [sqcot2, right1], [shape(blocks, F32)], flops=work)
     sqcot1, back1 = call(
-        functools.partial(chained_kernel, terms, scale),
-        [tl, tr, tf, receive_index, send_index],
+        with_terms(chained_kernel, terms, groups, scale), [tab, row, named, send_index],
         [density_guess, square1, right0, local2, returned2],
         [shape(blocks, BF16), shape(slots, BF16)],
         common + [pltpu.VMEM((blocks, width, width), BF16)], flops=3 * work)
     returned1 = exchange(back1)
-    (local1,) = call(local, [tl, tr], [sqcot1, right0], [shape(blocks, F32)], flops=work)
+    (local1,) = call(local, [tab], [sqcot1, right0], [shape(blocks, F32)], flops=work)
     (grad,) = call(final_kernel, [send_index], [local1, returned1], [shape(blocks, F32)])
     return (second, grad)
 

time: 204 us -> 199 us (0.975)
  local copies, waits for them, and re-layouts: 7.76 us -> 4.31 us
    unnamed x10 -> x8, local copies, waits for them, and re-layouts: 5.36 us -> 2.65 us
where the time goes in v4:
time: 199 us
  Pallas kernels  95.9 us (48%)
  waiting for transfers between devices  83.7 us (42%)
  starting transfers between devices  11.3 us (6%)
  local copies, waits for them, and re-layouts  4.31 us (2%)
  other arithmetic  3.02 us (2%)
    all_to_all x2, waiting for transfers between devices, exchange(): return lax.all_to_all(x, 'row', split_axis=0, concat_axis=0, tiled=True)  83.7 us
    pallas_call x1, Pallas kernels, spread_all(): pl.pallas_call(functools.partial(spread_kernel, nz, ny, nc, parts), out_s...  50.4 us
    pallas_call x6, Pallas kernels, call(): pl.pallas_call(kernel, out_shape=outs, in_specs=[smem] * len(prefetch) +...  45.5 us
    all_to_all x2, starting transfers between devices, exchange(): return lax.all_to_all(x, 'row', split_axis=0, concat_axis=0, tiled=True)  11.3 us
  transfers between devices with their start and end apart: 2, of which 2 were waited for; matrix products, arithmetic and copies ran while one was open for 1% of the time, Pallas kernels for 5%

profile of v4, /device:TPU:15, one launch (start us, length us, event | category | flops | bytes accessed | tf_op | source)
XLA Modules:
  0.0 198.9 jit_solution(6624157031910422758)
XLA Ops:
  0.6 0.7 broadcast_multiply_fusion
  1.3 0.7 pad_add_fusion
  2.0 0.1 copy.10
  2.1 0.1 broadcast_in_dim.24
  2.2 1.3 add.8.rest_1_
  3.4 0.6 broadcast_in_dim.25.own_tab.tab
  4.0 50.4 %shard_map.77 = (bf16[256,128,128]{2,1,0:T(8,128)(2,1)}, s32[16,8,128]{2,1,0:T(8,128)}) custom-call(bf16[16,128,128]{2,1,0:T(8,128)(2,1)} %rest_3_.1, s32[8,128]{1,0:T(8,128)} %broadcast_in_dim.25.own_tab.tab), custom_call_target="tpu_custom_call" | custom-call | tf_op jit(solution)/shard_map/pallas_call | solution.py:341
  54.4 23.4 %shard_map.78 = (bf16[16,128,128]{2,1,0:T(8,128)(2,1)}, bf16[16,128,128]{2,1,0:T(8,128)(2,1)}, bf16[32,128,128]{2,1,0:T(8,128)(2,1)}, bf16[32,128,128]{2,1,0:T(8...) custom-call(s32[8,128]{1,0:T(8,128)} %broadcast_in_dim.25.own_tab.tab, ...), custom_call_target="tpu_custom_call" | custom-call | flops 5905580032 | bytes 8912896 | tf_op jit(solution)/shard_map/pallas_call | solution.py:397
  77.9 0.0 copy-start.3
  77.9 0.0 copy-start.2
  77.9 6.5 %all-to-all-start = ((bf16[64,128,128]{2,1,0:T(8,128)(2,1)}), bf16[64,128,128]{2,1,0:T(8,128)(2,1)S(1)}, u32[]{:S(2)}, u32[]{:S(2)}) async-start(bf16[64,128,128]{2,1,0:T(8,128)(2,1)} %get-tuple-element.25), calls=%async_computation | async-start | bytes 4194304 | tf_op jit(solution)/shard_map/all_to_all | solution.py:424
  84.3 0.0 copy-done.3
  84.4 0.1 eq.32
  84.5 0.0 copy-done.2
  84.5 0.1 broadcast_in_dim.26
  84.5 0.2 reduce_window_sum.11
  84.7 0.2 select_reduce_fusion
  84.9 0.1 copy.11
  85.0 0.7 reshape.35.rest_2_.index
  85.6 3.5 %shard_map.80.rest_6_ = f32[16,128,128]{2,1,0:T(8,128)} custom-call(s32[8,128]{1,0:T(8,128)} %broadcast_in_dim.25.own_tab.tab, bf16[16,128,128]{2,1,0:T(8,128)(2,1)} %get-tuple-element.24.rest_0_, bf16[32,128,128]{2,1,0:T(8,128)(2,1)} %get-tuple-element.18.rest_1_), custom_call_target="tpu_custom_call" | custom-call | flops 268435456 | bytes 1572864 | tf_op jit(solution)/shard_map/pallas_call | solution.py:397
  89.1 42.6 %all-to-all-done.rest_7_ = bf16[64,128,128]{2,1,0:T(8,128)(2,1)S(1)} async-done(((bf16[64,128,128]{2,1,0:T(8,128)(2,1)}), bf16[64,128,128]{2,1,0:T(8,128)(2,1)S(1)}, u32[]{:S(2)}, u32[]{:S(2)}) %all-to-all-start) | async-done | bytes 2097184 | tf_op jit(solution)/shard_map/all_to_all | solution.py:424
  131.8 0.0 copy-start
  131.8 1.3 copy-done
  133.1 8.7 %shard_map.81 = (bf16[16,128,128]{2,1,0:T(8,128)(2,1)}, bf16[64,128,128]{2,1,0:T(8,128)(2,1)}) custom-call(s32[8,128]{1,0:T(8,128)} %broadcast_in_dim.25.own_tab.tab, s32[1]{0:T(128)} %bitcast.rest_0_, s32[512]{0:T(512)} %add.8.rest_1_, s32[64]{0:T(128)} %reshape.35.rest_2_.index, bf16[16,128,128]{2,1,0:T(8,128)(2,1)} %rest_3_.1, ...), custom_call_target="tpu_custom_call" | custom-call | flops 805306368 | bytes 5242880 | tf_op jit(solution)/shard_map/pallas_call | solution.py:397
  141.8 4.9 %all-to-all-start.1 = ((bf16[64,128,128]{2,1,0:T(8,128)(2,1)}), bf16[64,128,128]{2,1,0:T(8,128)(2,1)S(1)}, u32[]{:S(2)}, u32[]{:S(2)}) async-start(bf16[64,128,128]{2,1,0:T(8,128)(2,1)} %get-tuple-element.27), calls=%async_computation.1 | async-start | bytes 4194304 | tf_op jit(solution)/shard_map/all_to_all | solution.py:424
  146.6 2.9 %shard_map.79 = bf16[16,128,128]{2,1,0:T(8,128)(2,1)} custom-call(s32[8,128]{1,0:T(8,128)} %broadcast_in_dim.25.own_tab.tab, bf16[16,128,128]{2,1,0:T(8,128)(2,1)} %get-tuple-element.17.rest_0_, bf16[32,128,128]{2,1,0:T(8,128)(2,1)} %get-tuple-element.18.rest_1_), custom_call_target="tpu_custom_call" | custom-call | flops 268435456 | bytes 1572864 | tf_op jit(solution)/shard_map/pallas_call | solution.py:397
  149.5 3.5 %shard_map.82.local = f32[16,128,128]{2,1,0:T(8,128)} custom-call(s32[8,128]{1,0:T(8,128)} %broadcast_in_dim.25.own_tab.tab, bf16[16,128,128]{2,1,0:T(8,128)(2,1)} %get-tuple-element.26.rest_0_, bf16[32,128,128]{2,1,0:T(8,128)(2,1)} %get-tuple-element.23.rest_5_.rest_1_), custom_call_target="tpu_custom_call" | custom-call | flops 268435456 | bytes 1572864 | tf_op jit(solution)/shard_map/pallas_call | solution.py:397
  153.0 41.0 %all-to-all-done.1.returned = bf16[64,128,128]{2,1,0:T(8,128)(2,1)S(1)} async-done(((bf16[64,128,128]{2,1,0:T(8,128)(2,1)}), bf16[64,128,128]{2,1,0:T(8,128)(2,1)S(1)}, u32[]{:S(2)}, u32[]{:S(2)}) %all-to-all-start.1) | async-done | bytes 2097184 | tf_op jit(solution)/shard_map/all_to_all | solution.py:424
  194.0 0.0 copy-start.1
  194.0 1.3 copy-done.1
  195.4 3.5 %shard_map.83 = f32[16,128,128]{2,1,0:T(8,128)} custom-call(s32[64]{0:T(128)} %reshape.35.rest_2_.index, f32[16,128,128]{2,1,0:T(8,128)} %shard_map.82.local, bf16[64,128,128]{2,1,0:T(8,128)(2,1)} %copy-done.1), custom_call_target="tpu_custom_call" | custom-call | bytes 3145728 | tf_op jit(solution)/shard_map/pallas_call | solution.py:397
  (3 shorter events, 0.0 us)
Async XLA Ops:
  77.9 6.5 %copy-start.3 = (s32[512,1]{0,1:T(1,128)S(1)}, s32[512,1]{0,1:T(1,128)}, u32[]{:S(2)}) copy-start(s32[512,1]{0,1:T(1,128)} %param.10) | copy-start | bytes 6148
  77.9 6.6 %copy-start.2 = (s32[512]{0:T(512)S(1)}, s32[512]{0:T(512)}, u32[]{:S(2)}) copy-start(s32[512]{0:T(512)} %param.11) | copy-start | bytes 6148
  77.9 53.9 %all-to-all-start = ((bf16[64,128,128]{2,1,0:T(8,128)(2,1)}), bf16[64,128,128]{2,1,0:T(8,128)(2,1)S(1)}, u32[]{:S(2)}, u32[]{:S(2)}) async-start(bf16[64,128,128]{2,1,0:T(8,128)(2,1)} %get-tuple-element.25), calls=%async_computation | async-start | bytes 4194304 | tf_op jit(solution)/shard_map/all_to_all | solution.py:424
  131.8 1.3 copy-start
  141.8 52.3 %all-to-all-start.1 = ((bf16[64,128,128]{2,1,0:T(8,128)(2,1)}), bf16[64,128,128]{2,1,0:T(8,128)(2,1)S(1)}, u32[]{:S(2)}, u32[]{:S(2)}) async-start(bf16[64,128,128]{2,1,0:T(8,128)(2,1)} %get-tuple-element.27), calls=%async_computation.1 | async-start | bytes 4194304 | tf_op jit(solution)/shard_map/all_to_all | solution.py:424
  194.0 1.3 copy-start.1

commit v5 on v4

--- a/solution.py
+++ b/solution.py
@@ -10,6 +10,7 @@
 F32 = jnp.float32
 BF16 = jnp.bfloat16
 VMEM_LIMIT = 56 * 1024 * 1024
+LANDINGS = 4
 GATHER_BYTES = 16 * 1024 * 1024
 
 
@@ -98,13 +99,18 @@
     gather_kernel(index, fresh, out)
 
 
-def cot_phase(terms, scale, tl, tr, tf, row, blk, dens, square, right, cot, sqcot, sendback, acc, cube, both, racc, counts):
+def turn(dens, square, both):
+    @pl.loop(0, dens.shape[0], unroll=8)
+    def _(b):
+        both[b] = jnp.concatenate([square[b].T, dens[b].T], axis=1)
+
+
+def cot_phase(terms, scale, tl, tr, tf, row, blk, dens, right, cot, sqcot, sendback, acc, cube, both, racc, counts):
     blocks, width = dens.shape[0], dens.shape[2]
 
     @pl.loop(0, blocks, unroll=4)
     def _(b):
         cube[b] = (-2.0 * cot[b].astype(F32)).astype(BF16)
-        both[b] = jnp.concatenate([square[b].T, dens[b].T], axis=1)
 
     left_adjoint(cube, right, tl, tr, acc, terms)
 
@@ -143,20 +149,36 @@
 
 def reverse_kernel(terms, scale, tl, tr, tf, row, blk, dens, right, cot, square, sqcot, sendback, acc, cube, both, racc, counts):
     square_phase(terms, scale, tl, tr, tf, dens, right, square)
-    cot_phase(terms, scale, tl, tr, tf, row, blk, dens, square, right, cot, sqcot, sendback, acc, cube, both, racc, counts)
-
-
-def collect(index, returned, grad):
-    @pl.loop(0, returned.shape[0], unroll=8)
-    def _(s):
-        grad[index[s]] += returned[s].astype(F32)
-
-
-def chained_kernel(terms, scale, tl, tr, tf, row, blk, index, dens, square, right, local, returned, sqcot, sendback, acc, cube, both, racc, counts, cot):
-    acc[...] = local[...]
-    collect(index, returned, acc)
+    turn(dens, square, both)
+    cot_phase(terms, scale, tl, tr, tf, row, blk, dens, right, cot, sqcot, sendback, acc, cube, both, racc, counts)
+
+
+def collect(index, returned, landing, sems, grad, before):
+    size = returned.shape[0] // LANDINGS
+
+    def fetch(i):
+        span = pl.ds(i * size, size)
+        return pltpu.make_async_copy(returned.at[span], landing.at[span], sems.at[i])
+
+    for i in range(LANDINGS):
+        fetch(i).start()
+    before()
+    for i in range(LANDINGS):
+        fetch(i).wait()
+
+        @pl.loop(0, size, unroll=8)
+        def _(s):
+            grad[index[i * size + s]] += landing[i * size + s].astype(F32)
+
+
+def chained_kernel(terms, scale, tl, tr, tf, row, blk, index, dens, square, right, local, returned, sqcot, sendback, acc, cube, both, racc, counts, cot, landing, sems):
+    def before():
+        acc[...] = local[...]
+        turn(dens, square, both)
+
+    collect(index, returned, landing, sems, acc, before)
     cot[...] = acc[...].astype(BF16)
-    cot_phase(terms, scale, tl, tr, tf, row, blk, dens, square, right, cot, sqcot, sendback, acc, cube, both, racc, counts)
+    cot_phase(terms, scale, tl, tr, tf, row, blk, dens, right, cot, sqcot, sendback, acc, cube, both, racc, counts)
 
 
 def local_kernel(terms, scale, tl, tr, tf, sqcot, right, grad):
@@ -164,9 +186,11 @@
     grad[...] = scale * grad[...]
 
 
-def final_kernel(index, local, returned, grad):
-    grad[...] = local[...]
-    collect(index, returned, grad)
+def final_kernel(index, local, returned, grad, landing, sems):
+    def before():
+        grad[...] = local[...]
+
+    collect(index, returned, landing, sems, grad, before)
 
 
 def spread_kernel(nz, ny, nc, parts, own, own_tab, spread, tabs, send_sem, recv_sem, own_sem):
@@ -370,7 +394,7 @@
         rhs = jnp.concatenate([whole[i] for i in rights], axis=0)
         return scale * dot(lhs, rhs)
 
-    @pl.loop(0, requests, unroll=2)
+    @pl.loop(0, requests, unroll=4)
     def _(q):
         b = blk[me * requests + q]
         right0[q] = whole[b]
@@ -390,14 +414,14 @@
     reverse_kernel(terms, scale, tl, tr, tf, row, blk, fresh, right1, cot, square2, sqcot, sendback, acc, cube, both, racc, counts)
 
 
-def call(kernel, prefetch, arrays, outs, scratch=(), flops=0):
+def call(kernel, prefetch, arrays, outs, scratch=(), flops=0, left_out=0):
     whole = pl.BlockSpec(memory_space=pltpu.VMEM)
     smem = pl.BlockSpec(memory_space=pltpu.SMEM)
     moved = sum(a.size * a.dtype.itemsize for a in arrays)
     return pl.pallas_call(
         kernel,
         out_shape=outs,
-        in_specs=[smem] * len(prefetch) + [whole] * len(arrays),
+        in_specs=[smem] * len(prefetch) + [whole] * (len(arrays) - left_out) + [pl.BlockSpec(memory_space=pltpu.HBM)] * left_out,
         out_specs=[whole] * len(outs),
         scratch_shapes=list(scratch),
         cost_estimate=pl.CostEstimate(flops=flops, bytes_accessed=moved, transcendentals=0),
@@ -431,6 +455,8 @@
         pltpu.VMEM((request_count, width, width), F32),
         pltpu.SMEM((peer_count,), jnp.int32),
     ]
+
+    landing = [pltpu.VMEM((slots, width, width), BF16), pltpu.SemaphoreType.DMA((LANDINGS,))]
 
     def packed(*columns):
         tab = jnp.concatenate(columns, axis=1).reshape(1, -1)
@@ -472,10 +498,10 @@
         with_terms(chained_kernel, terms, groups, scale), [tab, row, named, send_index],
         [density_guess, square1, right0, local2, returned2],
         [shape(blocks, BF16), shape(slots, BF16)],
-        common + [pltpu.VMEM((blocks, width, width), BF16)], flops=3 * work)
+        common + [pltpu.VMEM((blocks, width, width), BF16)] + landing, flops=3 * work, left_out=1)
     returned1 = exchange(back1)
     (local1,) = call(local, [tab], [sqcot1, right0], [shape(blocks, F32)], flops=work)
-    (grad,) = call(final_kernel, [send_index], [local1, returned1], [shape(blocks, F32)])
+    (grad,) = call(final_kernel, [send_index], [local1, returned1], [shape(blocks, F32)], landing, left_out=1)
     return (second, grad)
 
 

time: 199 us -> 199 us (level)
  no operation moved by 1% of the time
where the time goes in v5:
time: 199 us; the launch traced here: 198 us
  Pallas kernels  95 us (48%)
  waiting for transfers between devices  83.7 us (42%)
  starting transfers between devices  11.4 us (6%)
  local copies, waits for them, and re-layouts  4.31 us (2%)
  other arithmetic  3.02 us (2%)
    all_to_all x2, waiting for transfers between devices, exchange(): return lax.all_to_all(x, 'row', split_axis=0, concat_axis=0, tiled=True)  83.7 us
    pallas_call x1, Pallas kernels, spread_all(): pl.pallas_call(functools.partial(spread_kernel, nz, ny, nc, parts), out_s...  50.4 us
    pallas_call x6, Pallas kernels, call(): pl.pallas_call(kernel, out_shape=outs, in_specs=[smem] * len(prefetch) +...  44.6 us
    all_to_all x2, starting transfers between devices, exchange(): return lax.all_to_all(x, 'row', split_axis=0, concat_axis=0, tiled=True)  11.4 us
  transfers between devices with their start and end apart: 2, of which 2 were waited for; matrix products, arithmetic and copies ran while one was open for 1% of the time, Pallas kernels for 5%

profile of v5, /device:TPU:15, one launch (start us, length us, event | category | flops | bytes accessed | tf_op | source)
XLA Modules:
  0.0 198.0 jit_solution(13056608585385622290)
XLA Ops:
  0.6 0.7 broadcast_multiply_fusion
  1.3 0.7 pad_add_fusion
  2.0 0.1 copy.10
  2.1 0.1 broadcast_in_dim.24
  2.2 1.3 add.8.rest_1_
  3.4 0.6 broadcast_in_dim.25.own_tab.tab
  4.0 50.4 %shard_map.77 = (bf16[256,128,128]{2,1,0:T(8,128)(2,1)}, s32[16,8,128]{2,1,0:T(8,128)}) custom-call(bf16[16,128,128]{2,1,0:T(8,128)(2,1)} %rest_3_.1, s32[8,128]{1,0:T(8,128)} %broadcast_in_dim.25.own_tab.tab), custom_call_target="tpu_custom_call" | custom-call | tf_op jit(solution)/shard_map/pallas_call | solution.py:365
  54.4 22.1 %shard_map.78 = (bf16[16,128,128]{2,1,0:T(8,128)(2,1)}, bf16[16,128,128]{2,1,0:T(8,128)(2,1)}, bf16[32,128,128]{2,1,0:T(8,128)(2,1)}, bf16[32,128,128]{2,1,0:T(8...) custom-call(s32[8,128]{1,0:T(8,128)} %broadcast_in_dim.25.own_tab.tab, ...), custom_call_target="tpu_custom_call" | custom-call | flops 5905580032 | bytes 8912896 | tf_op jit(solution)/shard_map/pallas_call | solution.py:421
  76.6 0.0 copy-start.3
  76.6 0.0 copy-start.2
  76.6 6.5 %all-to-all-start = ((bf16[64,128,128]{2,1,0:T(8,128)(2,1)}), bf16[64,128,128]{2,1,0:T(8,128)(2,1)S(1)}, u32[]{:S(2)}, u32[]{:S(2)}) async-start(bf16[64,128,128]{2,1,0:T(8,128)(2,1)} %get-tuple-element.25), calls=%async_computation | async-start | bytes 4194304 | tf_op jit(solution)/shard_map/all_to_all | solution.py:448
  83.1 0.0 copy-done.3
  83.1 0.1 eq.32
  83.2 0.0 copy-done.2
  83.2 0.1 broadcast_in_dim.26
  83.3 0.2 reduce_window_sum.11
  83.5 0.2 select_reduce_fusion
  83.6 0.1 copy.11
  83.7 0.7 reshape.35.rest_2_.index
  84.4 3.5 %shard_map.80.rest_6_ = f32[16,128,128]{2,1,0:T(8,128)} custom-call(s32[8,128]{1,0:T(8,128)} %broadcast_in_dim.25.own_tab.tab, bf16[16,128,128]{2,1,0:T(8,128)(2,1)} %get-tuple-element.24.rest_0_, bf16[32,128,128]{2,1,0:T(8,128)(2,1)} %get-tuple-element.18.rest_1_), custom_call_target="tpu_custom_call" | custom-call | flops 268435456 | bytes 1572864 | tf_op jit(solution)/shard_map/pallas_call | solution.py:421
  87.8 42.6 %all-to-all-done.rest_7_ = bf16[64,128,128]{2,1,0:T(8,128)(2,1)S(1)} async-done(((bf16[64,128,128]{2,1,0:T(8,128)(2,1)}), bf16[64,128,128]{2,1,0:T(8,128)(2,1)S(1)}, u32[]{:S(2)}, u32[]{:S(2)}) %all-to-all-start) | async-done | bytes 2097184 | tf_op jit(solution)/shard_map/all_to_all | solution.py:448
  130.5 0.0 copy-start
  130.5 1.3 copy-done
  131.8 8.7 %shard_map.81 = (bf16[16,128,128]{2,1,0:T(8,128)(2,1)}, bf16[64,128,128]{2,1,0:T(8,128)(2,1)}) custom-call(s32[8,128]{1,0:T(8,128)} %broadcast_in_dim.25.own_tab.tab, s32[1]{0:T(128)} %bitcast.rest_0_, s32[512]{0:T(512)} %add.8.rest_1_, s32[64]{0:T(128)} %reshape.35.rest_2_.index, bf16[16,128,128]{2,1,0:T(8,128)(2,1)} %rest_3_.1, ...), custom_call_target="tpu_custom_call" | custom-call | flops 805306368 | bytes 5242880 | tf_op jit(solution)/shard_map/pallas_call | solution.py:421
  140.5 4.9 %all-to-all-start.1 = ((bf16[64,128,128]{2,1,0:T(8,128)(2,1)}), bf16[64,128,128]{2,1,0:T(8,128)(2,1)S(1)}, u32[]{:S(2)}, u32[]{:S(2)}) async-start(bf16[64,128,128]{2,1,0:T(8,128)(2,1)} %get-tuple-element.27), calls=%async_computation.1 | async-start | bytes 4194304 | tf_op jit(solution)/shard_map/all_to_all | solution.py:448
  145.4 2.9 %shard_map.79 = bf16[16,128,128]{2,1,0:T(8,128)(2,1)} custom-call(s32[8,128]{1,0:T(8,128)} %broadcast_in_dim.25.own_tab.tab, bf16[16,128,128]{2,1,0:T(8,128)(2,1)} %get-tuple-element.17.rest_0_, bf16[32,128,128]{2,1,0:T(8,128)(2,1)} %get-tuple-element.18.rest_1_), custom_call_target="tpu_custom_call" | custom-call | flops 268435456 | bytes 1572864 | tf_op jit(solution)/shard_map/pallas_call | solution.py:421
  148.3 3.5 %shard_map.82.local = f32[16,128,128]{2,1,0:T(8,128)} custom-call(s32[8,128]{1,0:T(8,128)} %broadcast_in_dim.25.own_tab.tab, bf16[16,128,128]{2,1,0:T(8,128)(2,1)} %get-tuple-element.26.rest_0_, bf16[32,128,128]{2,1,0:T(8,128)(2,1)} %get-tuple-element.23.rest_5_.rest_1_), custom_call_target="tpu_custom_call" | custom-call | flops 268435456 | bytes 1572864 | tf_op jit(solution)/shard_map/pallas_call | solution.py:421
  151.8 41.0 %all-to-all-done.1.returned = bf16[64,128,128]{2,1,0:T(8,128)(2,1)S(1)} async-done(((bf16[64,128,128]{2,1,0:T(8,128)(2,1)}), bf16[64,128,128]{2,1,0:T(8,128)(2,1)S(1)}, u32[]{:S(2)}, u32[]{:S(2)}) %all-to-all-start.1) | async-done | bytes 2097184 | tf_op jit(solution)/shard_map/all_to_all | solution.py:448
  192.8 0.0 copy-start.1
  192.8 1.3 copy-done.1
  194.2 3.9 %shard_map.83 = f32[16,128,128]{2,1,0:T(8,128)} custom-call(s32[64]{0:T(128)} %reshape.35.rest_2_.index, f32[16,128,128]{2,1,0:T(8,128)} %shard_map.82.local, bf16[64,128,128]{2,1,0:T(8,128)(2,1)} %copy-done.1), custom_call_target="tpu_custom_call" | custom-call | bytes 3145728 | tf_op jit(solution)/shard_map/pallas_call | solution.py:421
  (3 shorter events, 0.0 us)
Async XLA Ops:
  76.6 6.5 %copy-start.3 = (s32[512,1]{0,1:T(1,128)S(1)}, s32[512,1]{0,1:T(1,128)}, u32[]{:S(2)}) copy-start(s32[512,1]{0,1:T(1,128)} %param.10) | copy-start | bytes 6148
  76.6 6.6 %copy-start.2 = (s32[512]{0:T(512)S(1)}, s32[512]{0:T(512)}, u32[]{:S(2)}) copy-start(s32[512]{0:T(512)} %param.11) | copy-start | bytes 6148
  76.6 53.9 %all-to-all-start = ((bf16[64,128,128]{2,1,0:T(8,128)(2,1)}), bf16[64,128,128]{2,1,0:T(8,128)(2,1)S(1)}, u32[]{:S(2)}, u32[]{:S(2)}) async-start(bf16[64,128,128]{2,1,0:T(8,128)(2,1)} %get-tuple-element.25), calls=%async_computation | async-start | bytes 4194304 | tf_op jit(solution)/shard_map/all_to_all | solution.py:448
  130.5 1.3 copy-start
  140.5 52.3 %all-to-all-start.1 = ((bf16[64,128,128]{2,1,0:T(8,128)(2,1)}), bf16[64,128,128]{2,1,0:T(8,128)(2,1)S(1)}, u32[]{:S(2)}, u32[]{:S(2)}) async-start(bf16[64,128,128]{2,1,0:T(8,128)(2,1)} %get-tuple-element.27), calls=%async_computation.1 | async-start | bytes 4194304 | tf_op jit(solution)/shard_map/all_to_all | solution.py:448
  192.8 1.3 copy-start.1

commit v6 on v5

--- a/solution.py
+++ b/solution.py
@@ -1,4 +1,5 @@
 import functools
+import math
 
 import jax
 import jax.numpy as jnp
@@ -9,7 +10,7 @@
 
 F32 = jnp.float32
 BF16 = jnp.bfloat16
-VMEM_LIMIT = 56 * 1024 * 1024
+VMEM_SPARE = 4 * 1024 * 1024
 LANDINGS = 4
 GATHER_BYTES = 16 * 1024 * 1024
 
@@ -418,14 +419,17 @@
     whole = pl.BlockSpec(memory_space=pltpu.VMEM)
     smem = pl.BlockSpec(memory_space=pltpu.SMEM)
     moved = sum(a.size * a.dtype.itemsize for a in arrays)
+    held = [*arrays[:len(arrays) - left_out], *outs]
+    held += [s for s in scratch if getattr(s, "memory_space", None) == pltpu.VMEM]
+    room = sum(math.prod(a.shape) * jnp.dtype(a.dtype).itemsize for a in held) + VMEM_SPARE
     return pl.pallas_call(
         kernel,
         out_shape=outs,
-        in_specs=[smem] * len(prefetch) + [whole] * (len(arrays) - left_out) + [pl.BlockSpec(memory_space=pltpu.HBM)] * left_out,
+        in_specs=[smem] * len(prefetch) + [whole] * (len(arrays) - left_out) + [pl.BlockSpec(memory_space=pl.ANY)] * left_out,
         out_specs=[whole] * len(outs),
         scratch_shapes=list(scratch),
         cost_estimate=pl.CostEstimate(flops=flops, bytes_accessed=moved, transcendentals=0),
-        compiler_params=pltpu.CompilerParams(vmem_limit_bytes=VMEM_LIMIT),
+        compiler_params=pltpu.CompilerParams(vmem_limit_bytes=room),
     )(*prefetch, *arrays)
 
 

time: 199 us -> 204 us (1.025)
  local copies, waits for them, and re-layouts: 4.31 us -> 21.5 us
  Pallas kernels: 95 us -> 82 us
    unnamed x8 -> x46, local copies, waits for them, and re-layouts: 2.65 us -> 20.4 us
    pallas_call x6, Pallas kernels: 44.6 us -> 31.6 us  [call(): pl.pallas_call(kernel, out_shape=outs, in_specs=[smem] * len(prefetch) +...]
  transfers between devices with their start and end apart: 2 -> 2, of which waited for: 2 -> 2; matrix products, arithmetic and copies ran while one was open for 1% -> 0% of each run, Pallas kernels for 5% -> 3%
where the time goes in v6:
time: 204 us; the launch traced here: 203 us
  waiting for transfers between devices  85.4 us (42%)
  Pallas kernels  82 us (40%)
  local copies, waits for them, and re-layouts  21.5 us (11%)
  starting transfers between devices  11.3 us (6%)
  other arithmetic  2.45 us (1%)
    all_to_all x2, waiting for transfers between devices, exchange(): return lax.all_to_all(x, 'row', split_axis=0, concat_axis=0, tiled=True)  85.4 us
    pallas_call x1, Pallas kernels, spread_all(): pl.pallas_call(functools.partial(spread_kernel, nz, ny, nc, parts), out_s...  50.4 us
    pallas_call x6, Pallas kernels, call(): pl.pallas_call(kernel, out_shape=outs, in_specs=[smem] * len(prefetch) +...  31.6 us
    unnamed x46, local copies, waits for them, and re-layouts  20.4 us
    all_to_all x2, starting transfers between devices, exchange(): return lax.all_to_all(x, 'row', split_axis=0, concat_axis=0, tiled=True)  11.3 us
  transfers between devices with their start and end apart: 2, of which 2 were waited for; matrix products, arithmetic and copies ran while one was open for 0% of the time, Pallas kernels for 3%

profile of v6, /device:TPU:15, one launch (start us, length us, event | category | flops | bytes accessed | tf_op | source)
XLA Modules:
  0.0 203.4 jit_solution(347174030550918012)
XLA Ops:
  0.6 0.7 broadcast_multiply_fusion
  1.3 0.7 pad_add_fusion
  2.2 0.7 add.8.rest_1_
  3.5 50.4 %shard_map.77 = (bf16[256,128,128]{2,1,0:T(8,128)(2,1)}, s32[16,8,128]{2,1,0:T(8,128)}) custom-call(bf16[16,128,128]{2,1,0:T(8,128)(2,1)} %rest_3_.1, s32[8,128]{1,0:T(8,128)} %broadcast_in_dim.25.own_tab.tab), custom_call_target="tpu_custom_call" | custom-call | tf_op jit(solution)/shard_map/pallas_call | solution.py:366
  53.9 0.7 copy-done.16
  54.6 3.4 %copy-done.18 = bf16[256,128,128]{2,1,0:T(8,128)(2,1)S(1)} copy-done((bf16[256,128,128]{2,1,0:T(8,128)(2,1)S(1)}, bf16[256,128,128]{2,1,0:T(8,128)(2,1)}, u32[]{:S(2)}) %copy-start.18) | copy-done | bytes 8388632
  57.9 1.0 copy-done.19
  59.0 0.8 copy-done.20
  59.8 18.3 %shard_map.78 = (bf16[16,128,128]{2,1,0:T(8,128)(2,1)}, bf16[16,128,128]{2,1,0:T(8,128)(2,1)S(1)}, bf16[32,128,128]{2,1,0:T(8,128)(2,1)S(1)}, bf16[32,128,128]{2...) custom-call(s32[8,128]{1,0:T(8,128)S(1)} %copy-done.16, ...), custom_call_target="tpu_custom_call" | custom-call | flops 5905580032 | bytes 8912896 | tf_op jit(solution)/shard_map/pallas_call | solution.py:425
  78.2 1.0 copy-done
  79.1 1.3 copy-done.6
  80.5 0.8 copy-done.8
  81.2 0.8 copy-done.10
  82.0 0.8 copy-done.14
  82.8 6.5 %all-to-all-start = ((bf16[64,128,128]{2,1,0:T(8,128)(2,1)}), bf16[64,128,128]{2,1,0:T(8,128)(2,1)S(1)}, u32[]{:S(2)}, u32[]{:S(2)}) async-start(bf16[64,128,128]{2,1,0:T(8,128)(2,1)} %copy-done.6), calls=%async_computation | async-start | bytes 4194304 | tf_op jit(solution)/shard_map/all_to_all | solution.py:452
  90.0 1.0 copy-done.11
  91.1 1.7 shard_map.80.rest_6_
  92.8 1.0 copy-done.3
  93.8 43.0 %all-to-all-done.rest_7_ = bf16[64,128,128]{2,1,0:T(8,128)(2,1)S(1)} async-done(((bf16[64,128,128]{2,1,0:T(8,128)(2,1)}), bf16[64,128,128]{2,1,0:T(8,128)(2,1)S(1)}, u32[]{:S(2)}, u32[]{:S(2)}) %all-to-all-start) | async-done | bytes 2097184 | tf_op jit(solution)/shard_map/all_to_all | solution.py:452
  136.7 1.2 copy-done.1
  137.9 1.2 copy-done.4
  139.2 1.0 copy-done.5
  140.2 1.0 copy-done.9
  141.2 5.5 %shard_map.81 = (bf16[16,128,128]{2,1,0:T(8,128)(2,1)S(1)}, bf16[64,128,128]{2,1,0:T(8,128)(2,1)S(1)}) custom-call(s32[8,128]{1,0:T(8,128)S(1)} %copy-done.17, s32[1]{0:T(128)} %bitcast.rest_0_, s32[512]{0:T(512)S(1)} %add.8.rest_1_, s32[64]{0:T(128)S(1)} %reshape.35.rest_2_.index, bf16[16,128,128]{2,1,0:T(8,128)(2,1)S(1)} %copy-done.5, ...), custom_call_target="tpu_custom_call" | custom-call | flops 805306368 | bytes 5242880 | tf_op jit(solution)/shard_map/pallas_call | solution.py:425
  146.8 1.3 copy-done.7
  148.1 0.8 copy-done.12
  148.9 4.9 %all-to-all-start.1 = ((bf16[64,128,128]{2,1,0:T(8,128)(2,1)}), bf16[64,128,128]{2,1,0:T(8,128)(2,1)S(1)}, u32[]{:S(2)}, u32[]{:S(2)}) async-start(bf16[64,128,128]{2,1,0:T(8,128)(2,1)} %copy-done.7), calls=%async_computation.1 | async-start | bytes 4194304 | tf_op jit(solution)/shard_map/all_to_all | solution.py:452
  153.8 1.1 copy-done.15
  154.9 2.1 %shard_map.79 = bf16[16,128,128]{2,1,0:T(8,128)(2,1)} custom-call(s32[8,128]{1,0:T(8,128)S(1)} %copy-done.17, bf16[16,128,128]{2,1,0:T(8,128)(2,1)S(1)} %copy-done.15, bf16[32,128,128]{2,1,0:T(8,128)(2,1)S(1)} %get-tuple-element.18.rest_1_), custom_call_target="tpu_custom_call" | custom-call | flops 268435456 | bytes 1572864 | tf_op jit(solution)/shard_map/pallas_call | solution.py:425
  157.1 1.7 shard_map.82.local
  158.8 42.4 %all-to-all-done.1.returned = bf16[64,128,128]{2,1,0:T(8,128)(2,1)S(1)} async-done(((bf16[64,128,128]{2,1,0:T(8,128)(2,1)}), bf16[64,128,128]{2,1,0:T(8,128)(2,1)S(1)}, u32[]{:S(2)}, u32[]{:S(2)}) %all-to-all-start.1) | async-done | bytes 2097184 | tf_op jit(solution)/shard_map/all_to_all | solution.py:452
  201.2 2.3 %shard_map.83 = f32[16,128,128]{2,1,0:T(8,128)} custom-call(s32[64]{0:T(128)S(1)} %reshape.35.rest_2_.index, f32[16,128,128]{2,1,0:T(8,128)S(1)} %shard_map.82.local, bf16[64,128,128]{2,1,0:T(8,128)(2,1)S(1)} %all-to-all-done.1.returned), custom_call_target="tpu_custom_call" | custom-call | bytes 3145728 | tf_op jit(solution)/shard_map/pallas_call | solution.py:425
  (40 shorter events, 1.5 us)
Async XLA Ops:
  53.9 0.7 copy-start.16
  54.6 3.4 %copy-start.18 = (bf16[256,128,128]{2,1,0:T(8,128)(2,1)S(1)}, bf16[256,128,128]{2,1,0:T(8,128)(2,1)}, u32[]{:S(2)}) copy-start(bf16[256,128,128]{2,1,0:T(8,128)(2,1)} %get-tuple-element.16.rest_3_) | copy-start | bytes 25165828
  57.9 1.0 copy-start.19
  59.0 0.8 copy-start.20
  78.2 1.0 copy-start
  79.1 1.3 copy-start.6
  80.5 0.8 copy-start.8
  81.2 0.8 copy-start.10
  82.0 0.8 copy-start.14
  82.8 6.5 %copy-start.22 = (s32[512,1]{0,1:T(1,128)S(1)}, s32[512,1]{0,1:T(1,128)}, u32[]{:S(2)}) copy-start(s32[512,1]{0,1:T(1,128)} %param.10) | copy-start | bytes 6148
  82.8 6.6 %copy-start.21 = (s32[512]{0:T(512)S(1)}, s32[512]{0:T(512)}, u32[]{:S(2)}) copy-start(s32[512]{0:T(512)} %param.11) | copy-start | bytes 6148
  82.8 7.2 %copy-start.17 = (s32[8,128]{1,0:T(8,128)S(1)}, s32[8,128]{1,0:T(8,128)}, u32[]{:S(2)}) copy-start(s32[8,128]{1,0:T(8,128)} %broadcast_in_dim.25.own_tab.tab) | copy-start | bytes 12292
  82.8 53.9 %all-to-all-start = ((bf16[64,128,128]{2,1,0:T(8,128)(2,1)}), bf16[64,128,128]{2,1,0:T(8,128)(2,1)S(1)}, u32[]{:S(2)}, u32[]{:S(2)}) async-start(bf16[64,128,128]{2,1,0:T(8,128)(2,1)} %copy-done.6), calls=%async_computation | async-start | bytes 4194304 | tf_op jit(solution)/shard_map/all_to_all | solution.py:452
  90.0 1.0 copy-start.11
  92.8 1.0 copy-start.3
  136.7 1.2 copy-start.1
  137.9 1.2 copy-start.4
  139.2 1.0 copy-start.5
  140.2 1.0 copy-start.9
  146.8 1.3 copy-start.7
  148.1 0.8 copy-start.12
  148.9 52.3 %all-to-all-start.1 = ((bf16[64,128,128]{2,1,0:T(8,128)(2,1)}), bf16[64,128,128]{2,1,0:T(8,128)(2,1)S(1)}, u32[]{:S(2)}, u32[]{:S(2)}) async-start(bf16[64,128,128]{2,1,0:T(8,128)(2,1)} %copy-done.7), calls=%async_computation.1 | async-start | bytes 4194304 | tf_op jit(solution)/shard_map/all_to_all | solution.py:452
  153.7 3.3 %copy-start.2 = (bf16[32,128,128]{2,1,0:T(8,128)(2,1)S(1)}, bf16[32,128,128]{2,1,0:T(8,128)(2,1)}, u32[]{:S(2)}) copy-start(bf16[32,128,128]{2,1,0:T(8,128)(2,1)} %copy-done) | copy-start | bytes 3145732
  153.8 3.3 %copy-start.13 = (bf16[16,128,128]{2,1,0:T(8,128)(2,1)S(1)}, bf16[16,128,128]{2,1,0:T(8,128)(2,1)}, u32[]{:S(2)}) copy-start(bf16[16,128,128]{2,1,0:T(8,128)(2,1)} %copy-done.12) | copy-start | bytes 1572868
  153.8 1.2 copy-start.15

commit v7 on v6

--- a/solution.py
+++ b/solution.py
@@ -10,6 +10,7 @@
 
 F32 = jnp.float32
 BF16 = jnp.bfloat16
+VMEM_LIMIT = 56 * 1024 * 1024
 VMEM_SPARE = 4 * 1024 * 1024
 LANDINGS = 4
 GATHER_BYTES = 16 * 1024 * 1024
@@ -415,7 +416,7 @@
     reverse_kernel(terms, scale, tl, tr, tf, row, blk, fresh, right1, cot, square2, sqcot, sendback, acc, cube, both, racc, counts)
 
 
-def call(kernel, prefetch, arrays, outs, scratch=(), flops=0, left_out=0):
+def call(kernel, prefetch, arrays, outs, scratch=(), flops=0, left_out=0, tight=False):
     whole = pl.BlockSpec(memory_space=pltpu.VMEM)
     smem = pl.BlockSpec(memory_space=pltpu.SMEM)
     moved = sum(a.size * a.dtype.itemsize for a in arrays)
@@ -429,7 +430,7 @@
         out_specs=[whole] * len(outs),
         scratch_shapes=list(scratch),
         cost_estimate=pl.CostEstimate(flops=flops, bytes_accessed=moved, transcendentals=0),
-        compiler_params=pltpu.CompilerParams(vmem_limit_bytes=room),
+        compiler_params=pltpu.CompilerParams(vmem_limit_bytes=room if tight else VMEM_LIMIT),
     )(*prefetch, *arrays)
 
 
@@ -505,7 +506,7 @@
         common + [pltpu.VMEM((blocks, width, width), BF16)] + landing, flops=3 * work, left_out=1)
     returned1 = exchange(back1)
     (local1,) = call(local, [tab], [sqcot1, right0], [shape(blocks, F32)], flops=work)
-    (grad,) = call(final_kernel, [send_index], [local1, returned1], [shape(blocks, F32)], landing, left_out=1)
+    (grad,) = call(final_kernel, [send_index], [local1, returned1], [shape(blocks, F32)], landing, left_out=1, tight=True)
     return (second, grad)
 
 

time: 204 us -> 197 us (0.966)
  local copies, waits for them, and re-layouts: 21.5 us -> 4.23 us
  Pallas kernels: 82 us -> 93.4 us
    unnamed x46 -> x10, local copies, waits for them, and re-layouts: 20.4 us -> 2.55 us
    pallas_call x6, Pallas kernels: 31.6 us -> 43 us  [call(): pl.pallas_call(kernel, out_shape=outs, in_specs=[smem] * len(prefetch) +...]
  transfers between devices with their start and end apart: 2 -> 2, of which waited for: 2 -> 2; matrix products, arithmetic and copies ran while one was open for 0% -> 1% of each run, Pallas kernels for 3% -> 5%
where the time goes in v7:
time: 197 us; the launch traced here: 196 us
  Pallas kernels  93.4 us (47%)
  waiting for transfers between devices  83.6 us (42%)
  starting transfers between devices  11.3 us (6%)
  local copies, waits for them, and re-layouts  4.23 us (2%)
  other arithmetic  2.98 us (2%)
    all_to_all x2, waiting for transfers between devices, exchange(): return lax.all_to_all(x, 'row', split_axis=0, concat_axis=0, tiled=True)  83.6 us
    pallas_call x1, Pallas kernels, spread_all(): pl.pallas_call(functools.partial(spread_kernel, nz, ny, nc, parts), out_s...  50.4 us
    pallas_call x6, Pallas kernels, call(): pl.pallas_call(kernel, out_shape=outs, in_specs=[smem] * len(prefetch) +...  43 us
    all_to_all x2, starting transfers between devices, exchange(): return lax.all_to_all(x, 'row', split_axis=0, concat_axis=0, tiled=True)  11.3 us
  transfers between devices with their start and end apart: 2, of which 2 were waited for; matrix products, arithmetic and copies ran while one was open for 1% of the time, Pallas kernels for 5%

profile of v7, /device:TPU:15, one launch (start us, length us, event | category | flops | bytes accessed | tf_op | source)
XLA Modules:
  0.0 196.3 jit_solution(3024805786430461911)
XLA Ops:
  0.6 0.7 broadcast_multiply_fusion
  1.3 0.7 pad_add_fusion
  2.0 0.1 copy.10
  2.1 0.1 broadcast_in_dim.24
  2.2 1.2 add.8.rest_1_
  3.4 0.6 broadcast_in_dim.25.own_tab.tab
  4.0 50.4 %shard_map.77 = (bf16[256,128,128]{2,1,0:T(8,128)(2,1)}, s32[16,8,128]{2,1,0:T(8,128)}) custom-call(bf16[16,128,128]{2,1,0:T(8,128)(2,1)} %rest_3_.1, s32[8,128]{1,0:T(8,128)} %broadcast_in_dim.25.own_tab.tab), custom_call_target="tpu_custom_call" | custom-call | tf_op jit(solution)/shard_map/pallas_call | solution.py:367
  54.4 22.1 %shard_map.78 = (bf16[16,128,128]{2,1,0:T(8,128)(2,1)}, bf16[16,128,128]{2,1,0:T(8,128)(2,1)}, bf16[32,128,128]{2,1,0:T(8,128)(2,1)}, bf16[32,128,128]{2,1,0:T(8...) custom-call(s32[8,128]{1,0:T(8,128)} %broadcast_in_dim.25.own_tab.tab, ...), custom_call_target="tpu_custom_call" | custom-call | flops 5905580032 | bytes 8912896 | tf_op jit(solution)/shard_map/pallas_call | solution.py:426
  76.5 0.0 copy-start.4
  76.5 0.0 copy-start.3
  76.5 6.4 %all-to-all-start = ((bf16[64,128,128]{2,1,0:T(8,128)(2,1)}), bf16[64,128,128]{2,1,0:T(8,128)(2,1)S(1)}, u32[]{:S(2)}, u32[]{:S(2)}) async-start(bf16[64,128,128]{2,1,0:T(8,128)(2,1)} %get-tuple-element.25), calls=%async_computation | async-start | bytes 4194304 | tf_op jit(solution)/shard_map/all_to_all | solution.py:453
  83.0 0.0 copy-done.4
  83.0 0.1 eq.32
  83.1 0.0 copy-done.3
  83.1 0.1 broadcast_in_dim.26
  83.2 0.2 reduce_window_sum.11
  83.4 0.2 select_reduce_fusion
  83.5 0.1 copy.11
  83.6 0.7 reshape.35.rest_2_.index
  84.3 3.5 %shard_map.80.rest_6_ = f32[16,128,128]{2,1,0:T(8,128)} custom-call(s32[8,128]{1,0:T(8,128)} %broadcast_in_dim.25.own_tab.tab, bf16[16,128,128]{2,1,0:T(8,128)(2,1)} %get-tuple-element.24.rest_0_, bf16[32,128,128]{2,1,0:T(8,128)(2,1)} %get-tuple-element.18.rest_1_), custom_call_target="tpu_custom_call" | custom-call | flops 268435456 | bytes 1572864 | tf_op jit(solution)/shard_map/pallas_call | solution.py:426
  87.8 42.6 %all-to-all-done.rest_7_ = bf16[64,128,128]{2,1,0:T(8,128)(2,1)S(1)} async-done(((bf16[64,128,128]{2,1,0:T(8,128)(2,1)}), bf16[64,128,128]{2,1,0:T(8,128)(2,1)S(1)}, u32[]{:S(2)}, u32[]{:S(2)}) %all-to-all-start) | async-done | bytes 2097184 | tf_op jit(solution)/shard_map/all_to_all | solution.py:453
  130.4 0.0 copy-start.2
  130.4 1.3 copy-done.2
  131.7 8.7 %shard_map.81 = (bf16[16,128,128]{2,1,0:T(8,128)(2,1)}, bf16[64,128,128]{2,1,0:T(8,128)(2,1)}) custom-call(s32[8,128]{1,0:T(8,128)} %broadcast_in_dim.25.own_tab.tab, s32[1]{0:T(128)} %bitcast.rest_0_, s32[512]{0:T(512)} %add.8.rest_1_, s32[64]{0:T(128)} %reshape.35.rest_2_.index, bf16[16,128,128]{2,1,0:T(8,128)(2,1)} %rest_3_.1, ...), custom_call_target="tpu_custom_call" | custom-call | flops 805306368 | bytes 5242880 | tf_op jit(solution)/shard_map/pallas_call | solution.py:426
  140.4 4.9 %all-to-all-start.1 = ((bf16[64,128,128]{2,1,0:T(8,128)(2,1)}), bf16[64,128,128]{2,1,0:T(8,128)(2,1)S(1)}, u32[]{:S(2)}, u32[]{:S(2)}) async-start(bf16[64,128,128]{2,1,0:T(8,128)(2,1)} %get-tuple-element.27), calls=%async_computation.1 | async-start | bytes 4194304 | tf_op jit(solution)/shard_map/all_to_all | solution.py:453
  145.3 0.0 copy-start.1
  145.3 2.9 %shard_map.79 = bf16[16,128,128]{2,1,0:T(8,128)(2,1)} custom-call(s32[8,128]{1,0:T(8,128)} %broadcast_in_dim.25.own_tab.tab, bf16[16,128,128]{2,1,0:T(8,128)(2,1)} %get-tuple-element.17.rest_0_, bf16[32,128,128]{2,1,0:T(8,128)(2,1)} %get-tuple-element.18.rest_1_), custom_call_target="tpu_custom_call" | custom-call | flops 268435456 | bytes 1572864 | tf_op jit(solution)/shard_map/pallas_call | solution.py:426
  148.3 3.5 %shard_map.82.local = f32[16,128,128]{2,1,0:T(8,128)} custom-call(s32[8,128]{1,0:T(8,128)} %broadcast_in_dim.25.own_tab.tab, bf16[16,128,128]{2,1,0:T(8,128)(2,1)} %get-tuple-element.26.rest_0_, bf16[32,128,128]{2,1,0:T(8,128)(2,1)} %get-tuple-element.23.rest_5_.rest_1_), custom_call_target="tpu_custom_call" | custom-call | flops 268435456 | bytes 1572864 | tf_op jit(solution)/shard_map/pallas_call | solution.py:426
  151.7 41.0 %all-to-all-done.1.returned = bf16[64,128,128]{2,1,0:T(8,128)(2,1)S(1)} async-done(((bf16[64,128,128]{2,1,0:T(8,128)(2,1)}), bf16[64,128,128]{2,1,0:T(8,128)(2,1)S(1)}, u32[]{:S(2)}, u32[]{:S(2)}) %all-to-all-start.1) | async-done | bytes 2097184 | tf_op jit(solution)/shard_map/all_to_all | solution.py:453
  192.8 0.0 copy-done.1
  192.8 1.2 copy-done
  194.0 2.3 %shard_map.83 = f32[16,128,128]{2,1,0:T(8,128)} custom-call(s32[64]{0:T(128)S(1)} %copy-done.1, f32[16,128,128]{2,1,0:T(8,128)S(1)} %copy-done, bf16[64,128,128]{2,1,0:T(8,128)(2,1)S(1)} %all-to-all-done.1.returned), custom_call_target="tpu_custom_call" | custom-call | bytes 3145728 | tf_op jit(solution)/shard_map/pallas_call | solution.py:426
  (4 shorter events, 0.0 us)
Async XLA Ops:
  76.5 6.4 %copy-start.4 = (s32[512,1]{0,1:T(1,128)S(1)}, s32[512,1]{0,1:T(1,128)}, u32[]{:S(2)}) copy-start(s32[512,1]{0,1:T(1,128)} %param.10) | copy-start | bytes 6148
  76.5 6.6 %copy-start.3 = (s32[512]{0:T(512)S(1)}, s32[512]{0:T(512)}, u32[]{:S(2)}) copy-start(s32[512]{0:T(512)} %param.11) | copy-start | bytes 6148
  76.5 53.9 %all-to-all-start = ((bf16[64,128,128]{2,1,0:T(8,128)(2,1)}), bf16[64,128,128]{2,1,0:T(8,128)(2,1)S(1)}, u32[]{:S(2)}, u32[]{:S(2)}) async-start(bf16[64,128,128]{2,1,0:T(8,128)(2,1)} %get-tuple-element.25), calls=%async_computation | async-start | bytes 4194304 | tf_op jit(solution)/shard_map/all_to_all | solution.py:453
  130.4 1.3 copy-start.2
  140.4 52.3 %all-to-all-start.1 = ((bf16[64,128,128]{2,1,0:T(8,128)(2,1)}), bf16[64,128,128]{2,1,0:T(8,128)(2,1)S(1)}, u32[]{:S(2)}, u32[]{:S(2)}) async-start(bf16[64,128,128]{2,1,0:T(8,128)(2,1)} %get-tuple-element.27), calls=%async_computation.1 | async-start | bytes 4194304 | tf_op jit(solution)/shard_map/all_to_all | solution.py:453
  145.3 47.4 %copy-start.1 = (s32[64]{0:T(128)S(1)}, s32[64]{0:T(128)}, u32[]{:S(2)}) copy-start(s32[64]{0:T(128)} %reshape.35.rest_2_.index) | copy-start | bytes 772
  192.8 1.2 copy-start

commit v8 on v7

--- a/solution.py
+++ b/solution.py
@@ -505,7 +505,7 @@
         [shape(blocks, BF16), shape(slots, BF16)],
         common + [pltpu.VMEM((blocks, width, width), BF16)] + landing, flops=3 * work, left_out=1)
     returned1 = exchange(back1)
-    (local1,) = call(local, [tab], [sqcot1, right0], [shape(blocks, F32)], flops=work)
+    (local1,) = call(local, [tab], [sqcot1, right0], [shape(blocks, F32)], flops=work, tight=True)
     (grad,) = call(final_kernel, [send_index], [local1, returned1], [shape(blocks, F32)], landing, left_out=1, tight=True)
     return (second, grad)
 

time: 197 us -> 195 us (0.990)
  transfers between devices with their start and end apart: 2 -> 2, of which waited for: 2 -> 2; matrix products, arithmetic and copies ran while one was open for 1% -> 1% of each run, Pallas kernels for 5% -> 4%
where the time goes in v8:
time: 195 us
  Pallas kernels  91.6 us (47%)
  waiting for transfers between devices  85.3 us (44%)
  starting transfers between devices  11.4 us (6%)
  local copies, waits for them, and re-layouts  3 us (2%)
  other arithmetic  2.99 us (2%)
    all_to_all x2, waiting for transfers between devices, exchange(): return lax.all_to_all(x, 'row', split_axis=0, concat_axis=0, tiled=True)  85.3 us
    pallas_call x1, Pallas kernels, spread_all(): pl.pallas_call(functools.partial(spread_kernel, nz, ny, nc, parts), out_s...  50.4 us
    pallas_call x6, Pallas kernels, call(): pl.pallas_call(kernel, out_shape=outs, in_specs=[smem] * len(prefetch) +...  41.2 us
    all_to_all x2, starting transfers between devices, exchange(): return lax.all_to_all(x, 'row', split_axis=0, concat_axis=0, tiled=True)  11.4 us
  transfers between devices with their start and end apart: 2, of which 2 were waited for; matrix products, arithmetic and copies ran while one was open for 1% of the time, Pallas kernels for 4%

profile of v8, /device:TPU:15, one launch (start us, length us, event | category | flops | bytes accessed | tf_op | source)
XLA Modules:
  0.0 195.1 jit_solution(9372810340620567706)
XLA Ops:
  0.6 0.7 broadcast_multiply_fusion
  1.3 0.7 pad_add_fusion
  2.0 0.1 copy.10
  2.1 0.1 broadcast_in_dim.24
  2.2 1.2 add.8.rest_1_
  3.4 0.6 broadcast_in_dim.25.own_tab.tab
  4.0 50.4 %shard_map.77 = (bf16[256,128,128]{2,1,0:T(8,128)(2,1)}, s32[16,8,128]{2,1,0:T(8,128)}) custom-call(bf16[16,128,128]{2,1,0:T(8,128)(2,1)} %rest_3_.1, s32[8,128]{1,0:T(8,128)} %broadcast_in_dim.25.own_tab.tab), custom_call_target="tpu_custom_call" | custom-call | tf_op jit(solution)/shard_map/pallas_call | solution.py:367
  54.4 22.1 %shard_map.78 = (bf16[16,128,128]{2,1,0:T(8,128)(2,1)}, bf16[16,128,128]{2,1,0:T(8,128)(2,1)}, bf16[32,128,128]{2,1,0:T(8,128)(2,1)}, bf16[32,128,128]{2,1,0:T(8...) custom-call(s32[8,128]{1,0:T(8,128)} %broadcast_in_dim.25.own_tab.tab, ...), custom_call_target="tpu_custom_call" | custom-call | flops 5905580032 | bytes 8912896 | tf_op jit(solution)/shard_map/pallas_call | solution.py:426
  76.5 6.5 %all-to-all-start = ((bf16[64,128,128]{2,1,0:T(8,128)(2,1)}), bf16[64,128,128]{2,1,0:T(8,128)(2,1)S(1)}, u32[]{:S(2)}, u32[]{:S(2)}) async-start(bf16[64,128,128]{2,1,0:T(8,128)(2,1)} %get-tuple-element.25), calls=%async_computation | async-start | bytes 4194304 | tf_op jit(solution)/shard_map/all_to_all | solution.py:453
  83.0 0.0 copy-done.6
  83.1 0.1 eq.32
  83.2 0.0 copy-done.5
  83.2 0.1 broadcast_in_dim.26
  83.2 0.2 reduce_window_sum.11
  83.4 0.2 select_reduce_fusion
  83.6 0.1 copy.11
  83.7 0.7 reshape.35.rest_2_.index
  84.3 3.5 %shard_map.80.rest_6_ = f32[16,128,128]{2,1,0:T(8,128)} custom-call(s32[8,128]{1,0:T(8,128)} %broadcast_in_dim.25.own_tab.tab, bf16[16,128,128]{2,1,0:T(8,128)(2,1)} %get-tuple-element.24.rest_0_, bf16[32,128,128]{2,1,0:T(8,128)(2,1)} %get-tuple-element.18.rest_1_), custom_call_target="tpu_custom_call" | custom-call | flops 268435456 | bytes 1572864 | tf_op jit(solution)/shard_map/pallas_call | solution.py:426
  87.8 42.6 %all-to-all-done.rest_7_ = bf16[64,128,128]{2,1,0:T(8,128)(2,1)S(1)} async-done(((bf16[64,128,128]{2,1,0:T(8,128)(2,1)}), bf16[64,128,128]{2,1,0:T(8,128)(2,1)S(1)}, u32[]{:S(2)}, u32[]{:S(2)}) %all-to-all-start) | async-done | bytes 2097184 | tf_op jit(solution)/shard_map/all_to_all | solution.py:453
  130.4 1.3 copy-done.4
  131.7 8.7 %shard_map.81 = (bf16[16,128,128]{2,1,0:T(8,128)(2,1)}, bf16[64,128,128]{2,1,0:T(8,128)(2,1)}) custom-call(s32[8,128]{1,0:T(8,128)} %broadcast_in_dim.25.own_tab.tab, s32[1]{0:T(128)} %bitcast.rest_0_, s32[512]{0:T(512)} %add.8.rest_1_, s32[64]{0:T(128)} %reshape.35.rest_2_.index, bf16[16,128,128]{2,1,0:T(8,128)(2,1)} %rest_3_.1, ...), custom_call_target="tpu_custom_call" | custom-call | flops 805306368 | bytes 5242880 | tf_op jit(solution)/shard_map/pallas_call | solution.py:426
  140.5 4.9 %all-to-all-start.1 = ((bf16[64,128,128]{2,1,0:T(8,128)(2,1)}), bf16[64,128,128]{2,1,0:T(8,128)(2,1)S(1)}, u32[]{:S(2)}, u32[]{:S(2)}) async-start(bf16[64,128,128]{2,1,0:T(8,128)(2,1)} %get-tuple-element.27), calls=%async_computation.1 | async-start | bytes 4194304 | tf_op jit(solution)/shard_map/all_to_all | solution.py:453
  145.4 0.0 copy-start.1
  145.4 0.0 copy-start.2
  145.4 0.0 copy-start.3
  145.4 3.0 %shard_map.79 = bf16[16,128,128]{2,1,0:T(8,128)(2,1)} custom-call(s32[8,128]{1,0:T(8,128)} %broadcast_in_dim.25.own_tab.tab, bf16[16,128,128]{2,1,0:T(8,128)(2,1)} %get-tuple-element.17.rest_0_, bf16[32,128,128]{2,1,0:T(8,128)(2,1)} %get-tuple-element.18.rest_1_), custom_call_target="tpu_custom_call" | custom-call | flops 268435456 | bytes 1572864 | tf_op jit(solution)/shard_map/pallas_call | solution.py:426
  148.4 0.0 copy-done
  148.5 0.0 copy-done.1
  148.5 1.7 shard_map.82.local
  150.2 42.6 %all-to-all-done.1.returned = bf16[64,128,128]{2,1,0:T(8,128)(2,1)S(1)} async-done(((bf16[64,128,128]{2,1,0:T(8,128)(2,1)}), bf16[64,128,128]{2,1,0:T(8,128)(2,1)S(1)}, u32[]{:S(2)}, u32[]{:S(2)}) %all-to-all-start.1) | async-done | bytes 2097184 | tf_op jit(solution)/shard_map/all_to_all | solution.py:453
  192.8 0.0 copy-done.3
  192.8 2.2 %shard_map.83 = f32[16,128,128]{2,1,0:T(8,128)} custom-call(s32[64]{0:T(128)S(1)} %copy-done.3, f32[16,128,128]{2,1,0:T(8,128)S(1)} %shard_map.82.local, bf16[64,128,128]{2,1,0:T(8,128)(2,1)S(1)} %all-to-all-done.1.returned), custom_call_target="tpu_custom_call" | custom-call | bytes 3145728 | tf_op jit(solution)/shard_map/pallas_call | solution.py:426
  (8 shorter events, 0.0 us)
Async XLA Ops:
  76.5 6.5 %copy-start.6 = (s32[512,1]{0,1:T(1,128)S(1)}, s32[512,1]{0,1:T(1,128)}, u32[]{:S(2)}) copy-start(s32[512,1]{0,1:T(1,128)} %param.10) | copy-start | bytes 6148
  76.5 6.6 %copy-start.5 = (s32[512]{0:T(512)S(1)}, s32[512]{0:T(512)}, u32[]{:S(2)}) copy-start(s32[512]{0:T(512)} %param.11) | copy-start | bytes 6148
  76.5 53.9 %all-to-all-start = ((bf16[64,128,128]{2,1,0:T(8,128)(2,1)}), bf16[64,128,128]{2,1,0:T(8,128)(2,1)S(1)}, u32[]{:S(2)}, u32[]{:S(2)}) async-start(bf16[64,128,128]{2,1,0:T(8,128)(2,1)} %get-tuple-element.25), calls=%async_computation | async-start | bytes 4194304 | tf_op jit(solution)/shard_map/all_to_all | solution.py:453
  130.4 1.3 copy-start.4
  140.5 52.4 %all-to-all-start.1 = ((bf16[64,128,128]{2,1,0:T(8,128)(2,1)}), bf16[64,128,128]{2,1,0:T(8,128)(2,1)S(1)}, u32[]{:S(2)}, u32[]{:S(2)}) async-start(bf16[64,128,128]{2,1,0:T(8,128)(2,1)} %get-tuple-element.27), calls=%async_computation.1 | async-start | bytes 4194304 | tf_op jit(solution)/shard_map/all_to_all | solution.py:453
  145.4 3.1 %copy-start = (bf16[32,128,128]{2,1,0:T(8,128)(2,1)S(1)}, bf16[32,128,128]{2,1,0:T(8,128)(2,1)}, u32[]{:S(2)}) copy-start(bf16[32,128,128]{2,1,0:T(8,128)(2,1)} %get-tuple-element.23.rest_5_.rest_1_) | copy-start | bytes 3145732
  145.4 3.1 %copy-start.1 = (bf16[16,128,128]{2,1,0:T(8,128)(2,1)S(1)}, bf16[16,128,128]{2,1,0:T(8,128)(2,1)}, u32[]{:S(2)}) copy-start(bf16[16,128,128]{2,1,0:T(8,128)(2,1)} %get-tuple-element.26.rest_0_) | copy-start | bytes 1572868
  145.4 3.0 %copy-start.2 = (s32[8,128]{1,0:T(8,128)S(1)}, s32[8,128]{1,0:T(8,128)}, u32[]{:S(2)}) copy-start(s32[8,128]{1,0:T(8,128)} %broadcast_in_dim.25.own_tab.tab) | copy-start | bytes 12292
  145.4 47.4 %copy-start.3 = (s32[64]{0:T(128)S(1)}, s32[64]{0:T(128)}, u32[]{:S(2)}) copy-start(s32[64]{0:T(128)} %reshape.35.rest_2_.index) | copy-start | bytes 772
